TPU v7x, 256 devices: a whole 4x4x8 slice. The times are simulated.
256 devices in a mesh: ctx: 64 (over z, x, core), head: 4 (over y).
Axes of the slice: x: 4, y: 4, z: 8, core: 2. Of those that a mesh axis runs over, the one named last changes fastest.
Arguments:
- x_query: bfloat16 [16384, 4096], P('ctx', 'head'), may hold values from -6 to 6
- x_key: bfloat16 [16384, 4096], P('ctx', 'head'), may hold values from -6 to 6
- x_value: bfloat16 [16384, 4096], P('ctx', 'head'), may hold values from -6 to 6
- gate_logits: bfloat16 [16384, 4096], P('ctx', 'head'), may hold values from -6 to 6
- norm_gain: bfloat16 [4096], P('head'), may hold values from 0.099609375 to 1.8984375
- out_grad: bfloat16 [16384, 4096], P('ctx', 'head'), may hold values from -6 to 6
- doc_ids: int32 [16384], P('ctx'), may hold values from 0 to 31, never falling along the last dimension, each value on 1 to 1024 neighbouring positions
Outputs:
- attn_out: bfloat16 [16384, 4096], P('ctx', 'head')
- query_grad: bfloat16 [16384, 4096], P('ctx', 'head')
- key_grad: bfloat16 [16384, 4096], P('ctx', 'head')
- value_grad: bfloat16 [16384, 4096], P('ctx', 'head')
- gate_grad: bfloat16 [16384, 4096], P('ctx', 'head')
- gain_grad: float32 [4096], P('head')
Inputs may be any that keep to these rules, and one draw needn't show every extreme that they name: doc_ids never fall along the tokens; each document takes 1 to 1024 consecutive tokens, one exactly 1024.
All inputs are finite; a program needn't handle non-finite values.
Results may differ from a plain program's by a relative error of at most 0.0072.
Values sent between devices are 32-bit elements; how exact they have to be, the bound alone decides.
A program may use at most 128 MiB of HBM per device.

v0:
```python
import jax
import jax.numpy as jnp
from jax import lax
from jax.sharding import PartitionSpec as P

HD = 128


epsilon = 1e-06


def carried_in_2(array, axis, combine, identity, reverse):
    count, mine = (lax.axis_size(axis), lax.axis_index(axis))
    everything = jax.tree.map(lambda part: lax.all_gather(part, axis), array)
    start = jax.tree.map(
        lambda part, zero: jnp.broadcast_to(jnp.asarray(zero, part.dtype), part.shape),
        array,
        identity,
    )

    def hop(k, before):
        at = count - 1 - k if reverse else k
        reached = at > mine if reverse else at < mine
        new = combine(before, jax.tree.map(lambda part: part[at], everything))
        return jax.tree.map(lambda a, b: jnp.where(reached, a, b), new, before)

    return lax.fori_loop(0, count, hop, start)


def activate(raw):
    wide = raw.astype(jnp.float32)
    return (wide * jax.nn.sigmoid(wide)).astype(jnp.bfloat16)


def silu_slope(raw):
    wide = raw.astype(jnp.float32)
    logistic = jax.nn.sigmoid(wide)
    return logistic * (1.0 + wide * (1.0 - logistic))


def block_mask(labels):
    length = labels.shape[0]
    row_index = lax.broadcasted_iota(jnp.int32, (length, length), 0)
    col_index = lax.broadcasted_iota(jnp.int32, (length, length), 1)
    return (row_index >= col_index) & (labels[:, None] == labels[None, :])


def link(earlier, nearer):
    summed_far, doc_far, whole_far = earlier
    summed_near, doc_near, whole_near = nearer
    agrees = (doc_far == doc_near) | (doc_far < 0.0) | (doc_near < 0.0)
    absorb = (whole_near > 0.5) & agrees
    summed = summed_near + jnp.where(absorb, summed_far, jnp.zeros_like(summed_far))
    doc_key = jnp.where(doc_near < 0.0, doc_far, doc_near)
    whole = jnp.where(agrees, whole_far * whole_near, jnp.float32(0.0))
    return (summed, doc_key, whole)


def local(x_query, x_key, x_value, gate_logits, norm_gain, out_grad, doc_ids):
    length = x_query.shape[0]
    heads_here = x_query.shape[1] // HD
    features = heads_here * HD * lax.axis_size("head")
    split_shape = (length, heads_here, HD)
    flat_shape = (length, heads_here * HD)
    query_act = activate(x_query).reshape(split_shape)
    key_act = activate(x_key).reshape(split_shape)
    value_act = activate(x_value).reshape(split_shape)
    allowed = block_mask(doc_ids)
    first_doc = doc_ids[0]
    last_doc = doc_ids[-1]
    in_first = (doc_ids == first_doc)[:, None, None]
    in_last = (doc_ids == last_doc)[:, None, None]
    whole = jnp.where(first_doc == last_doc, jnp.float32(1.0), jnp.float32(0.0))
    neutral = (jnp.zeros((heads_here, HD, HD), jnp.float32), jnp.float32(-1.0), jnp.float32(1.0))
    scores = jnp.einsum("thd,shd->hts", query_act, key_act, preferred_element_type=jnp.float32)
    weights = jnp.where(allowed[None], scores, 0.0).astype(jnp.bfloat16)
    inside = jnp.einsum("hts,shd->thd", weights, value_act, preferred_element_type=jnp.float32)
    tail_keys = jnp.where(in_last, key_act, jnp.zeros_like(key_act))
    own_part = jnp.einsum("thd,the->hde", tail_keys, value_act, preferred_element_type=jnp.float32)
    element = (own_part, last_doc.astype(jnp.float32), whole)
    state_sum, state_doc, _ = carried_in_2(element, "ctx", link, neutral, False)
    incoming = jnp.where(
        state_doc == first_doc.astype(jnp.float32), state_sum, jnp.zeros_like(state_sum)
    )
    rounded_in = incoming.astype(jnp.bfloat16)
    carried_in = jnp.einsum(
        "thd,hde->the", query_act, rounded_in, preferred_element_type=jnp.float32
    )
    mixture = inside + jnp.where(in_first, carried_in, 0.0)
    squares = jnp.sum(mixture * mixture, axis=(1, 2))
    sum_rows = lax.psum(squares, "head")
    inv_rms = lax.rsqrt(sum_rows / features + epsilon)[:, None, None]
    gain_f32 = norm_gain.astype(jnp.float32).reshape(heads_here, HD)
    normed = mixture * inv_rms * gain_f32
    gate_open = jax.nn.sigmoid(gate_logits.astype(jnp.float32)).reshape(split_shape)
    attn_out = (normed * gate_open).astype(jnp.bfloat16).reshape(flat_shape)
    upstream = out_grad.astype(jnp.float32).reshape(split_shape)
    gate_grad = (
        (upstream * normed * gate_open * (1.0 - gate_open)).astype(jnp.bfloat16).reshape(flat_shape)
    )
    normed_grad = upstream * gate_open
    gain_part = jnp.sum(normed_grad * mixture * inv_rms, axis=0).reshape(heads_here * HD)
    gain_grad = lax.psum(gain_part, "ctx")
    row_inner = lax.psum(jnp.sum(gain_f32 * normed_grad * mixture, axis=(1, 2)), "head")[
        :, None, None
    ]
    cubed = inv_rms * inv_rms * inv_rms
    mix_grad = (gain_f32 * normed_grad * inv_rms - mixture * row_inner * cubed / features).astype(
        jnp.bfloat16
    )
    head_queries = jnp.where(in_first, query_act, jnp.zeros_like(query_act))
    grad_part = jnp.einsum(
        "thd,the->hde", head_queries, mix_grad, preferred_element_type=jnp.float32
    )
    back_element = (grad_part, first_doc.astype(jnp.float32), whole)
    grad_sum, grad_doc, _ = carried_in_2(back_element, "ctx", link, neutral, True)
    grad_in = jnp.where(
        grad_doc == last_doc.astype(jnp.float32), grad_sum, jnp.zeros_like(grad_sum)
    )
    rounded_grad = grad_in.astype(jnp.bfloat16)
    pair_scores = jnp.einsum(
        "thd,shd->hts", mix_grad, value_act, preferred_element_type=jnp.float32
    )
    pair_grad = jnp.where(allowed[None], pair_scores, 0.0).astype(jnp.bfloat16)
    query_part = jnp.einsum("hts,shd->thd", pair_grad, key_act, preferred_element_type=jnp.float32)
    query_part = query_part + jnp.where(
        in_first,
        jnp.einsum("the,hde->thd", mix_grad, rounded_in, preferred_element_type=jnp.float32),
        0.0,
    )
    key_part = jnp.einsum("hts,thd->shd", pair_grad, query_act, preferred_element_type=jnp.float32)
    key_part = key_part + jnp.where(
        in_last,
        jnp.einsum("the,hde->thd", value_act, rounded_grad, preferred_element_type=jnp.float32),
        0.0,
    )
    value_part = jnp.einsum("hts,thd->shd", weights, mix_grad, preferred_element_type=jnp.float32)
    value_part = value_part + jnp.where(
        in_last,
        jnp.einsum("thd,hde->the", key_act, rounded_grad, preferred_element_type=jnp.float32),
        0.0,
    )
    query_grad = (query_part.reshape(flat_shape) * silu_slope(x_query)).astype(jnp.bfloat16)
    key_grad = (key_part.reshape(flat_shape) * silu_slope(x_key)).astype(jnp.bfloat16)
    value_grad = (value_part.reshape(flat_shape) * silu_slope(x_value)).astype(jnp.bfloat16)
    return (attn_out, query_grad, key_grad, value_grad, gate_grad, gain_grad)


def solution(mesh):
    placed = (
        P("ctx", "head"),
        P("ctx", "head"),
        P("ctx", "head"),
        P("ctx", "head"),
        P("head"),
        P("ctx", "head"),
        P("ctx"),
    )
    return jax.shard_map(
        local,
        mesh=mesh,
        in_specs=placed,
        out_specs=(
            P("ctx", "head"),
            P("ctx", "head"),
            P("ctx", "head"),
            P("ctx", "head"),
            P("ctx", "head"),
            P("head"),
        ),
        check_vma=False,
    )
```

profile of v0, /device:TPU:1, one launch (start us, length us, event | category | flops | bytes accessed | tf_op | source)
XLA Modules:
  0.0 991.9 jit_solution(13010588163265927835)
XLA Ops:
  7.2 2.3 fusion.61
  10.6 1.3 broadcast_compare_fusion
  12.0 1.3 fusion.38
  16.8 1.3 add_divide_fusion
  18.1 1.6 copy.44
  21.6 130.2 %all-reduce.4 = (f32[64]{0:T(128)S(1)}, f32[64]{0:T(128)S(1)}) all-reduce(f32[64]{0:T(128)S(1)} %dynamic-update-slice, f32[64]{0:T(128)S(1)} %dynamic-update-slice.1), channel_id=1, replica_groups=mesh['ctx'=64,'head'=4] {'ctx'}, use_global_device_ids=true, to_apply=%add | all-reduce | flops 128 | bytes 1024
  152.0 1.6 select_convert_fusion.1
  154.5 1.5 fusion.34
  156.1 4.9 all-gather.5.cloned.1.call-done
  160.9 322.7 %while.34 = (s32[]{:T(128)}, f32[8,128,128]{2,1,0:T(8,128)S(1)}, f32[]{:T(128)}, s32[]{:T(128)}, f32[64,8,128,128]{3,2,1,0:T(8,128)}, /*index=5*/f32[64]{0:T(128...) while((s32[]{:T(128)}, f32[8,128,128]{2,1,0:T(8,128)S(1)}, ...), condition=%wide.region_1.2_spmd.clone, body=%wide.region_0.1_spmd.clone.sunk | while | flops 524301 | bytes 1573101 | solution.py:27
  164.1 1.2 fusion.88
  174.1 1.2 fusion.88
  179.2 1.2 fusion.88
  184.2 1.2 fusion.88
  194.3 1.2 fusion.88
  199.4 1.2 fusion.88
  214.5 1.2 fusion.88
  219.5 1.2 fusion.88
  234.7 1.2 fusion.88
  239.7 1.2 fusion.88
  254.8 1.2 fusion.88
  259.9 1.2 fusion.88
  269.9 1.2 fusion.88
  275.0 1.2 fusion.88
  280.0 1.2 fusion.88
  290.1 1.2 fusion.88
  295.2 1.2 fusion.88
  310.3 1.2 fusion.88
  315.3 1.2 fusion.88
  330.5 1.2 fusion.88
  335.5 1.2 fusion.88
  350.6 1.2 fusion.88
  355.7 1.2 fusion.88
  365.7 1.2 fusion.88
  370.8 1.2 fusion.88
  375.8 1.2 fusion.88
  385.9 1.2 fusion.88
  391.0 1.2 fusion.88
  406.1 1.2 fusion.88
  411.1 1.2 fusion.88
  426.3 1.2 fusion.88
  431.3 1.2 fusion.88
  446.4 1.2 fusion.88
  451.5 1.2 fusion.88
  461.5 1.2 fusion.88
  466.6 1.2 fusion.88
  471.6 1.2 fusion.88
  481.7 1.2 fusion.88
  483.6 2.6 multiply_reduce_fusion.2
  486.2 8.4 psum.21
  494.6 2.5 multiply_reduce_fusion
  497.1 6.0 psum.22
  503.1 2.5 subtract_convert_fusion
  508.4 1.7 select_convert_fusion
  510.7 1.3 fusion.4
  512.0 2.5 copy.50
  515.5 133.4 %all-reduce.3 = (f32[64]{0:T(128)S(1)}, f32[1024]{0:T(1024)}) all-reduce(f32[64]{0:T(128)S(1)} %dynamic-update-slice.2, f32[1024]{0:T(1024)S(1)} %bitcast.114), channel_id=1, replica_groups=mesh['ctx'=64,'head'=4] {'ctx'}, use_global_device_ids=true, to_apply=%add.2 | all-reduce | flops 1088 | bytes 8704
  648.9 1.6 fusion.65
  650.6 2.5 fusion.64
  654.3 323.1 %while.35 = (s32[]{:T(128)}, f32[8,128,128]{2,1,0:T(8,128)S(1)}, f32[]{:T(128)}, s32[]{:T(128)}, f32[64,8,128,128]{3,2,1,0:T(8,128)}, /*index=5*/f32[64]{0:T(128...) while((s32[]{:T(128)}, f32[8,128,128]{2,1,0:T(8,128)S(1)}, ...), condition=%wide.region_7.8_spmd.clone, body=%wide.region_6.7_spmd.clone.sunk | while | flops 524305 | bytes 1573163 | solution.py:27
  662.5 1.2 fusion.89
  978.9 2.7 fusion.5
  981.6 1.6 copy.55
  983.3 1.8 fusion.14
  (421 shorter events, 271.2 us)
Async XLA Ops:
  7.2 2.8 copy-start.20
  7.2 4.8 copy-start.16
  7.2 153.7 %all-gather.5.cloned.1.call-start = ((), (), s32[]{:S(2)}) async-start(), calls=%async_computation | async-start | bytes 34078720 | tf_op jit(solution)/shard_map/all_gather | solution.py:14
  9.9 3.3 copy-start.5
  11.9 4.1 copy-start.9
  13.3 3.3 copy-start.14
  13.3 3.5 copy-start.15
  13.3 641.0 %all-gather.7.cloned.1.call-start = ((), (), s32[]{:S(2)}) async-start(), calls=%async_computation.1 | async-start | bytes 34078720 | tf_op jit(solution)/shard_map/all_gather | solution.py:14
  16.6 467.1 %copy-start = (bf16[256,1024]{0,1:T(8,128)(2,1)}, bf16[256,1024]{0,1:T(8,128)(2,1)S(1)}, u32[]{:S(2)}) copy-start(bf16[256,1024]{0,1:T(8,128)(2,1)S(1)} %copy.66) | copy-start | bytes 1572868
  16.8 2.9 copy-start.22
  16.8 135.0 %copy-start.21 = (bf16[1024]{0:T(1024)(128)(2,1)S(1)}, bf16[1024]{0:T(1024)(128)(2,1)}, u32[]{:S(2)}) copy-start(bf16[1024]{0:T(1024)(128)(2,1)} %param.15) | copy-start | bytes 6148
  151.8 2.7 copy-start.17
  153.5 1.0 copy-start.13
  503.1 2.5 copy-start.1
  505.5 1.9 copy-start.7
  508.4 1.7 copy-start.6
  510.2 1.8 copy-start.3
  510.7 3.9 copy-start.12
  514.5 136.0 %copy-start.2 = (bf16[256,1024]{0,1:T(8,128)(2,1)S(1)}, bf16[256,1024]{0,1:T(8,128)(2,1)}, u32[]{:S(2)}) copy-start(bf16[256,1024]{0,1:T(8,128)(2,1)} %copy-done) | copy-start | bytes 1572868
  648.9 4.2 copy-start.4
  648.9 4.2 copy-start.10
  654.3 323.1 %copy-start.8 = (bf16[32,8,8,128]{3,2,1,0:T(8,128)(2,1)S(1)}, bf16[32,8,8,128]{3,2,1,0:T(8,128)(2,1)}, u32[]{:S(2)}) copy-start(bf16[32,8,8,128]{3,2,1,0:T(8,128)(2,1)} %get-tuple-element.410) | copy-start | bytes 1572868
  977.8 1.0 copy-start.18
  981.6 1.7 copy-start.11
  981.6 1.7 copy-start.19
Sparse Core Ops, SparseCore 0:
  13.4 147.4 all-gather.4
  506.8 143.6 all-gather.6
where the time goes:
time: 1000 us; the launch traced here: 992 us
  loops' own time  339 us (34%)
  blocking collectives  278 us (28%)
  other arithmetic  170 us (17%)
  local copies, waits for them, and re-layouts  164 us (16%)
  matrix products  18.9 us (2%)
  between operations  17.1 us (2%)
    another operation x2, loops' own time, carried_in_2(): return lax.fori_loop(0, count, hop, start)  339 us
    unnamed x2, blocking collectives  264 us
    select_n x128, other arithmetic, hop(): return jax.tree.map(lambda a, b: jnp.where(reached, a, b), new, before)  156 us
    dynamic_slice x256, local copies, waits for them, and re-layouts, hop(): new = combine(before, jax.tree.map(lambda part: part[at], everything))  150 us
  transfers between devices with their start and end apart: 2, of which 1 were waited for; matrix products, arithmetic and copies ran while one was open for 2% of the time, Pallas kernels for 0%

commit v1 on v0

v1 whole, which is shorter than its diff:
```python
import functools

import jax
import jax.numpy as jnp
from jax import lax
from jax.experimental import pallas as pl
from jax.experimental.pallas import tpu as pltpu
from jax.sharding import PartitionSpec as P

HD = 128
EPS = 1e-06
MESH = pl.DeviceIdType.MESH
F32 = jnp.float32
BF16 = jnp.bfloat16
XS, CORES = 4, 2


def mm(a, b, ca, cb):
    return lax.dot_general(a, b, (((ca,), (cb,)), ((), ())), preferred_element_type=F32)


def sigmoid(x):
    return 0.5 + 0.5 * jnp.tanh(0.5 * x)


def kernel(
    n_ctx, n_head, heads,
    xq_hbm, xk_hbm, xv_hbm, gl_hbm, og_hbm, gain_ref, doc_ref,
    attn_ref, qg_ref, kg_ref, vg_ref, gg_ref, gaing_ref,
    xq, xk, xv, gl, og,
    ka, va, qa, qf, kl, vl, mg,
    wts, mix, ng, gng, sg, kp, vp, sk, sv,
    lab, mask, acc, inv_b, cc_b,
    own, sib_out, sib_in, tsend, tin, st,
    meta, stat, gbuf,
    in_sem, sib_s, sib_r, far_s, far_r, meta_s, meta_r, stat_s, stat_r, gain_s, gain_r,
):
    half = heads // 2
    features = heads * HD * n_head
    c, y = lax.axis_index("ctx"), lax.axis_index("head")
    p = lax.rem(c, 2)
    g = c // 2
    chips = n_ctx // 2
    zs = n_ctx // (XS * CORES)
    z, x = c // (XS * CORES), lax.rem(g, XS)
    sibling = (g * 2 + 1 - p, y)

    def chip(d):
        return (lax.rem(g + d + chips, chips) * 2 + p, y)

    y_peers = [(c, lax.rem(y + d, n_head)) for d in range(1, n_head)]
    x_peers = [((z * XS + lax.rem(x + d, XS)) * 2 + p, y) for d in range(1, XS)]
    z_peers = [((lax.rem(z + d, zs) * XS + x) * 2 + p, y) for d in range(1, zs)]
    near = [chip(1), chip(2), chip(-1), chip(-2)]
    peers = [sibling] + near + y_peers + x_peers + z_peers

    loads = []
    for i, (src, dst) in enumerate(((xk_hbm, xk), (xv_hbm, xv), (xq_hbm, xq), (gl_hbm, gl), (og_hbm, og))):
        cp = pltpu.make_async_copy(src, dst, in_sem.at[i])
        cp.start()
        loads.append(cp)
    barrier = pltpu.get_barrier_semaphore()
    for q in peers:
        pl.semaphore_signal(barrier, inc=1, device_id=q, device_id_type=MESH)

    def remote(src, dst, ssem, rsem, dev):
        return pltpu.make_async_remote_copy(
            src_ref=src, dst_ref=dst, send_sem=ssem, recv_sem=rsem, device_id=dev, device_id_type=MESH
        )

    def loop(n, body):
        lax.fori_loop(0, n, lambda i, carry: (body(i), carry)[1], 0)

    def cols(h):
        return pl.ds(pl.multiple_of(h * HD, HD), HD)

    row = doc_ref[...].astype(F32)
    tokens = row.shape[1]
    lab[...] = jnp.broadcast_to(row, (HD, tokens)).T
    first, last = lab[0:1, :], lab[tokens - 1 : tokens, :]
    meta[0] = jnp.zeros(meta.shape[1:], F32)
    meta[2] = jnp.zeros(meta.shape[1:], F32)
    stat[0] = jnp.zeros(stat.shape[1:], F32)
    meta[0, 0:1, :] = first
    meta[0, 1:2, :] = last

    def own_part(h):
        s = cols(h)
        k = xk[:, s].astype(F32)
        v = xv[:, s].astype(F32)
        kb = (k * sigmoid(k)).astype(BF16)
        vb = (v * sigmoid(v)).astype(BF16)
        ka[:, s] = kb
        va[:, s] = vb
        in_last = lab[...] == lab[tokens - 1 : tokens, :]
        kb = jnp.where(in_last, kb.astype(F32), 0.0).astype(BF16)
        kl[:, s] = kb
        own[h] = mm(kb, vb, 0, 0)

    def sib_copy(d, i, src):
        return remote(src, sib_in.at[d, i], sib_s.at[d, i], sib_r.at[d, i], sibling)

    def far_copy(d, i, k):
        step = (k + 1) * (1 if d == 0 else -1)
        return remote(tsend.at[d, i], tin.at[d, k, i], far_s.at[d, k, i], far_r.at[d, k, i], chip(step))

    def meta_copy(k):
        if k == 0:
            return remote(meta.at[0], meta.at[1], meta_s.at[0], meta_r.at[0], sibling)
        return remote(meta.at[2], meta.at[2 + k], meta_s.at[k], meta_r.at[k], near[k - 1])

    loads[0].wait()
    loads[1].wait()
    mine = p * half
    other = (1 - p) * half
    own_part(other)
    pl.semaphore_wait(barrier, len(peers))
    meta_copy(0).start()
    sib_copy(0, 0, own.at[other]).start()

    def send_own(i):
        own_part(other + i + 1)
        sib_copy(0, i + 1, own.at[other + i + 1]).start()

    loop(half - 1, send_own)

    own_part(mine)
    meta_copy(0).wait_recv()
    lo = p == 0
    f_lo = jnp.where(lo, meta[0, 0:1, :], meta[1, 0:1, :])
    l_lo = jnp.where(lo, meta[0, 1:2, :], meta[1, 1:2, :])
    f_hi = jnp.where(lo, meta[1, 0:1, :], meta[0, 0:1, :])
    l_hi = jnp.where(lo, meta[1, 1:2, :], meta[0, 1:2, :])
    meta[2, 0:1, :] = f_lo
    meta[2, 1:2, :] = l_hi
    for k in range(1, 5):
        meta_copy(k).start()

    def send_total(i, d):
        a, b = own[mine + i], sib_in[d, i]
        lo_part, hi_part = jnp.where(lo, a, b), jnp.where(lo, b, a)
        if d == 0:
            total = hi_part + jnp.where(l_lo == l_hi, lo_part, 0.0)
        else:
            total = lo_part + jnp.where(f_lo == f_hi, hi_part, 0.0)
        tsend[d, i] = total
        far_copy(d, i, 0).start()
        far_copy(d, i, 1).start()

    def fwd_total(i):
        @pl.when(i > 0)
        def _():
            own_part(mine + i)

        sib_copy(0, i, own.at[other + i]).wait_recv()
        send_total(i, 0)

    loop(half, fwd_total)

    t_iota = lax.broadcasted_iota(jnp.int32, (tokens, tokens), 0)
    s_iota = lax.broadcasted_iota(jnp.int32, (tokens, tokens), 1)
    lab2 = jnp.concatenate([lab[...]] * (tokens // HD), axis=1)
    mask[...] = jnp.where((lab2 == row) & (t_iota >= s_iota), 1.0, 0.0)
    loads[2].wait()
    loads[3].wait()
    loads[4].wait()

    def inside(h):
        s = cols(h)
        q = xq[:, s].astype(F32)
        qb = (q * sigmoid(q)).astype(BF16)
        qa[:, s] = qb
        in_first = lab[...] == lab[0:1, :]
        qf[:, s] = jnp.where(in_first, qb.astype(F32), 0.0).astype(BF16)
        w = (mm(qb, ka[:, s], 1, 1) * mask[...]).astype(BF16)
        wts[h] = w
        mix[:, s] = mm(w, va[:, s], 1, 0)
        gate = sigmoid(gl[:, s].astype(F32))
        sg[:, s] = gate
        grad = og[:, s].astype(F32) * gate
        ng[:, s] = grad
        gng[:, s] = grad * gain_ref[:, s].astype(F32)
        v = xv[:, s].astype(F32)
        gv = sigmoid(v)
        sv[:, s] = gv * (1.0 + v * (1.0 - gv))
        k = xk[:, s].astype(F32)
        gk = sigmoid(k)
        sk[:, s] = gk * (1.0 + k * (1.0 - gk))
        in_last = lab[...] == lab[tokens - 1 : tokens, :]
        vl[:, s] = jnp.where(in_last, va[:, s].astype(F32), 0.0).astype(BF16)

    loop(heads, inside)
    acc[...] = jnp.zeros_like(acc)

    for k in range(1, 5):
        meta_copy(k).wait_recv()

    def receive(d, i, finish):
        far_copy(d, i, 0).wait_recv()
        far_copy(d, i, 1).wait_recv()
        a, b = own[mine + i], sib_in[d, i]
        lo_part, hi_part = jnp.where(lo, a, b), jnp.where(lo, b, a)
        if d == 0:
            near_ok, far_ok = meta[3, 1:2, :] == f_lo, meta[4, 1:2, :] == f_lo
            edge = jnp.where(near_ok, tin[d, 0, i], 0.0) + jnp.where(far_ok, tin[d, 1, i], 0.0)
            inner = jnp.where(l_lo == f_hi, lo_part, 0.0) + jnp.where(f_lo == f_hi, edge, 0.0)
            to_lo, to_hi = edge, inner
        else:
            near_ok, far_ok = meta[5, 0:1, :] == l_hi, meta[6, 0:1, :] == l_hi
            edge = jnp.where(near_ok, tin[d, 0, i], 0.0) + jnp.where(far_ok, tin[d, 1, i], 0.0)
            inner = jnp.where(f_hi == l_lo, hi_part, 0.0) + jnp.where(l_hi == l_lo, edge, 0.0)
            to_lo, to_hi = inner, edge
        sib_out[d, i] = jnp.where(lo, to_hi, to_lo)
        sib_copy(d, half + i, sib_out.at[d, i]).start()
        st[d, mine + i] = jnp.where(lo, to_lo, to_hi).astype(BF16)
        finish(mine + i)

    def receive_sib(d, i, finish):
        sib_copy(d, half + i, sib_out.at[d, i]).wait_recv()
        st[d, other + i] = sib_in[d, half + i].astype(BF16)
        finish(other + i)

    def mixture(h):
        s = cols(h)
        m = mix[:, s] + mm(qf[:, s], st[0, h], 1, 0)
        mix[:, s] = m
        acc[0] += m * m
        acc[1] += gng[:, s] * m

    loop(half, lambda i: receive(0, i, mixture))
    loop(half, lambda i: receive_sib(0, i, mixture))

    stat[0, 0:1, :] = jnp.sum(acc[0].T, axis=0, keepdims=True)
    stat[0, 1:2, :] = jnp.sum(acc[1].T, axis=0, keepdims=True)

    def stat_copy(k):
        return remote(stat.at[0], stat.at[1 + k], stat_s.at[k], stat_r.at[k], y_peers[k])

    for k in range(n_head - 1):
        stat_copy(k).start()
    for k in range(n_head - 1):
        stat_copy(k).wait_recv()
    rows = stat[0]
    for k in range(n_head - 1):
        rows = rows + stat[1 + k]
    inv = lax.rsqrt(rows[0:1, :] / features + EPS)
    cc = rows[1:2, :] * (inv * inv * inv) / features
    inv_b[...] = jnp.broadcast_to(inv, (HD, tokens)).T
    cc_b[...] = jnp.broadcast_to(cc, (HD, tokens)).T

    def grad_part(h):
        s = cols(h)
        m = (gng[:, s] * inv_b[...] - mix[:, s] * cc_b[...]).astype(BF16)
        mg[:, s] = m
        own[h] = mm(qf[:, s], m, 0, 0)

    for i in range(half):
        sib_copy(0, i, own.at[other + i]).wait_send()

    def send_grad(i):
        grad_part(other + i)
        sib_copy(1, i, own.at[other + i]).start()

    loop(half, send_grad)

    def bwd_total(i):
        grad_part(mine + i)
        sib_copy(1, i, own.at[other + i]).wait_recv()
        send_total(i, 1)

    loop(half, bwd_total)

    def tail(h):
        s = cols(h)
        unit = mix[:, s] * inv_b[...]
        gbuf[0, pl.ds(h, 1), :] = jnp.sum(ng[:, s] * unit, axis=0, keepdims=True)
        normed = unit * gain_ref[:, s].astype(F32)
        gate = sg[:, s]
        attn_ref[:, s] = (normed * gate).astype(BF16)
        gg_ref[:, s] = (ng[:, s] * normed * (1.0 - gate)).astype(BF16)

    loop(heads, tail)

    def gain_copy(slot, dst, k, dev):
        return remote(gbuf.at[slot], gbuf.at[dst], gain_s.at[k], gain_r.at[k], dev)

    core_copy = gain_copy(0, 3, 0, sibling)
    x_copies = [gain_copy(1, 4 + k, 1 + k, q) for k, q in enumerate(x_peers)]
    z_copies = [gain_copy(2, 4 + XS - 1 + k, XS + k, q) for k, q in enumerate(z_peers)]
    core_copy.start()

    def pair(h):
        s = cols(h)
        m = mg[:, s]
        w = wts[h]
        pg = (mm(m, va[:, s], 1, 1) * mask[...]).astype(BF16)
        vp[:, s] = mm(w, m, 0, 0)
        kp[:, s] = mm(pg, qa[:, s], 0, 0)
        q = xq[:, s].astype(F32)
        gq = sigmoid(q)
        slope = gq * (1.0 + q * (1.0 - gq))
        in_first = lab[...] == lab[0:1, :]
        part = mm(pg, ka[:, s], 1, 0) + jnp.where(in_first, mm(m, st[0, h], 1, 1), 0.0)
        qg_ref[:, s] = (part * slope).astype(BF16)

    pair(0)
    core_copy.wait_recv()
    gbuf[1] = gbuf[0] + gbuf[3]
    for cp in x_copies:
        cp.start()
    loop(half - 1, lambda i: pair(i + 1))
    total = gbuf[1]
    for k, cp in enumerate(x_copies):
        cp.wait_recv()
        total = total + gbuf[4 + k]
    gbuf[2] = total
    for cp in z_copies:
        cp.start()
    loop(half, lambda i: pair(half + i))

    def final(h):
        s = cols(h)
        gb = st[1, h]
        kg_ref[:, s] = ((kp[:, s] + mm(vl[:, s], gb, 1, 1)) * sk[:, s]).astype(BF16)
        vg_ref[:, s] = ((vp[:, s] + mm(kl[:, s], gb, 1, 0)) * sv[:, s]).astype(BF16)

    loop(half, lambda i: receive(1, i, final))
    total = gbuf[2]
    for k, cp in enumerate(z_copies):
        cp.wait_recv()
        total = total + gbuf[4 + XS - 1 + k]
    gaing_ref[...] = total
    loop(half, lambda i: receive_sib(1, i, final))

    for k in range(5):
        meta_copy(k).wait_send()
    for k in range(n_head - 1):
        stat_copy(k).wait_send()
    for cp in [core_copy] + x_copies + z_copies:
        cp.wait_send()

    def drain(i):
        sib_copy(1, i, own.at[other + i]).wait_send()
        for d in (0, 1):
            sib_copy(d, half + i, sib_out.at[d, i]).wait_send()
            far_copy(d, i, 0).wait_send()
            far_copy(d, i, 1).wait_send()

    loop(half, drain)


def local(n_ctx, n_head, x_query, x_key, x_value, gate_logits, norm_gain, out_grad, doc_ids):
    tokens, width = x_query.shape
    heads = width // HD
    half = heads // 2
    zs = n_ctx // (XS * CORES)
    flat16 = pltpu.VMEM((tokens, width), BF16)
    flat32 = pltpu.VMEM((tokens, width), F32)
    square = pltpu.VMEM((tokens, tokens), F32)
    thin = pltpu.VMEM((tokens, HD), F32)
    state = lambda *lead: pltpu.VMEM((*lead, HD, HD), F32)
    dma = pltpu.SemaphoreType.DMA
    n_gain = 1 + (XS - 1) + (zs - 1)
    vmem = pl.BlockSpec(memory_space=pltpu.VMEM)
    anywhere = pl.BlockSpec(memory_space=pl.ANY)
    big = jax.ShapeDtypeStruct((tokens, width), BF16)
    outs = pl.pallas_call(
        functools.partial(kernel, n_ctx, n_head, heads),
        out_shape=(big, big, big, big, big, jax.ShapeDtypeStruct((heads, HD), F32)),
        in_specs=[anywhere] * 5 + [vmem] * 2,
        out_specs=(vmem,) * 6,
        scratch_shapes=[flat16] * 5 + [flat16] * 7
        + [pltpu.VMEM((heads, tokens, tokens), BF16)] + [flat32] * 8
        + [thin, square, pltpu.VMEM((2, tokens, HD), F32), thin, thin]
        + [
            state(heads), state(2, half), state(2, 2 * half), state(2, half), state(2, 2, half),
            pltpu.VMEM((2, heads, HD, HD), BF16),
            pltpu.VMEM((7, 8, HD), F32),
            pltpu.VMEM((n_head, 8, tokens), F32),
            pltpu.VMEM((3 + n_gain, heads, HD), F32),
            dma((5,)), dma((2, 2 * half)), dma((2, 2 * half)), dma((2, 2, half)), dma((2, 2, half)),
            dma((5,)), dma((5,)), dma((n_head - 1,)), dma((n_head - 1,)), dma((n_gain,)), dma((n_gain,)),
        ],
        compiler_params=pltpu.CompilerParams(
            collective_id=0, has_side_effects=True, vmem_limit_bytes=56 << 20
        ),
        cost_estimate=pl.CostEstimate(flops=1 << 30, bytes_accessed=5 << 20, transcendentals=1 << 20),
    )(x_query, x_key, x_value, gate_logits, out_grad, norm_gain.reshape(1, width), doc_ids.reshape(1, tokens))
    return (*outs[:5], outs[5].reshape(width))


def solution(mesh):
    n_ctx, n_head = mesh.shape["ctx"], mesh.shape["head"]
    placed = (
        P("ctx", "head"), P("ctx", "head"), P("ctx", "head"), P("ctx", "head"),
        P("head"), P("ctx", "head"), P("ctx"),
    )
    return jax.shard_map(
        functools.partial(local, n_ctx, n_head),
        mesh=mesh,
        in_specs=placed,
        out_specs=(P("ctx", "head"),) * 5 + (P("head"),),
        check_vma=False,
    )
```

time: 1000 us -> 64 us (0.06)
  loops' own time: 339 us -> 0 us
  blocking collectives: 278 us -> 0 us
  other arithmetic: 170 us -> 0 us
  local copies, waits for them, and re-layouts: 164 us -> 8.29 us
  Pallas kernels: 0 us -> 54 us
  matrix products: 18.9 us -> 0 us
  between operations: 17.1 us -> 0.66 us
    another operation x2 -> x0, loops' own time: 339 us -> none  [carried_in_2(): return lax.fori_loop(0, count, hop, start)]
    unnamed x2 -> x0, blocking collectives: 264 us -> none
    select_n x128 -> x0, other arithmetic: 156 us -> none  [hop(): return jax.tree.map(lambda a, b: jnp.where(reached, a, b), new, before)]
    dynamic_slice x256 -> x0, local copies, waits for them, and re-layouts: 150 us -> none  [hop(): new = combine(before, jax.tree.map(lambda part: part[at], everything))]
    pallas_call x0 -> x1, Pallas kernels: none -> 54 us  [local(): pl.pallas_call(functools.partial(kernel, n_ctx, n_head, heads), out_shape...]
    dot_general x12 -> x0, matrix products: 18.9 us -> none  [the longest x1 2.75 us: local(): jnp.einsum('the,hde->thd', value_act, rounded_grad, preferred_element_typ...]
    psum x2 -> x0, blocking collectives: 14.4 us -> none  [the longest x1 8.41 us: local(): sum_rows = lax.psum(squares, 'head')]
  transfers between devices with their start and end apart: 2 -> 0, of which waited for: 1 -> 0; matrix products, arithmetic and copies ran while one was open for 2% -> 0% of each run, Pallas kernels for 0% -> 0%
where the time goes in v1:
time: 64 us; the launch traced here: 63 us
  Pallas kernels  54 us (84%)
  local copies, waits for them, and re-layouts  8.29 us (13%)
  between operations  0.66 us (1%)
    pallas_call x1, Pallas kernels, local(): pl.pallas_call(functools.partial(kernel, n_ctx, n_head, heads), out_shape...  54 us
    unnamed x16, local copies, waits for them, and re-layouts  7.01 us

profile of v1, /device:TPU:1, one launch (start us, length us, event | category | flops | bytes accessed | tf_op | source)
XLA Modules:
  0.0 63.0 jit_solution(545667209697061763)
XLA Ops:
  0.6 1.3 %reshape.21.gain_ref = bf16[1,1024]{1,0:T(2,128)(2,1)} reshape(bf16[1024]{0:T(1024)(128)(2,1)} %param.11) | data formatting | bytes 4096 | tf_op jit(solution)/shard_map/reshape | solution.py:388
  1.9 54.0 %shard_map.118 = (bf16[256,1024]{1,0:T(8,128)(2,1)}, bf16[256,1024]{1,0:T(8,128)(2,1)}, bf16[256,1024]{1,0:T(8,128)(2,1)}, bf16[256,1024]{1,0:T(8,128)(2,1)}, bf...) custom-call(bf16[256,1024]{1,0:T(8,128)(2,1)} %xq_hbm.1, bf16[256,1024]{1,0:T(8,128)(2,1)} %xk_hbm.1, bf16[256,1024]{1,0:T(8,128)(2,1)} %xv_hbm.1, ...), custom_call_target="tpu_custom_call" | custom-call | flops 1073741824 | bytes 5242880 | tf_op jit(solution)/shard_map/pallas_call | solution.py:367
  55.9 0.0 copy-start.3
  55.9 1.9 %copy.19 = bf16[256,1024]{1,0:T(8,128)(2,1)} copy(bf16[256,1024]{1,0:T(8,128)(2,1)} %get-tuple-element.24) | data formatting | bytes 1048576
  57.9 0.0 copy-done.3
  57.9 0.0 copy-start.2
  57.9 0.8 %copy.20 = bf16[256,1024]{1,0:T(8,128)(2,1)} copy(bf16[256,1024]{1,0:T(8,128)(2,1)S(1)} %copy-done.3) | data formatting | bytes 1048576
  58.7 0.4 copy-done.2
  59.1 0.0 copy-start.1
  59.1 0.8 %copy.21 = bf16[256,1024]{1,0:T(8,128)(2,1)} copy(bf16[256,1024]{1,0:T(8,128)(2,1)S(1)} %copy-done.2) | data formatting | bytes 1048576
  59.9 0.4 copy-done.1
  60.3 0.0 copy-start
  60.3 0.8 %copy.22 = bf16[256,1024]{1,0:T(8,128)(2,1)} copy(bf16[256,1024]{1,0:T(8,128)(2,1)S(1)} %copy-done.1) | data formatting | bytes 1048576
  61.1 0.4 copy-done
  61.6 0.0 copy-start.4
  61.6 0.8 %copy.23 = bf16[256,1024]{1,0:T(8,128)(2,1)} copy(bf16[256,1024]{1,0:T(8,128)(2,1)S(1)} %copy-done) | data formatting | bytes 1048576
  62.4 0.0 copy-done.4
  62.4 0.6 copy.24
Async XLA Ops:
  55.9 1.9 %copy-start.3 = (bf16[256,1024]{1,0:T(8,128)(2,1)S(1)}, bf16[256,1024]{1,0:T(8,128)(2,1)}, u32[]{:S(2)}) copy-start(bf16[256,1024]{1,0:T(8,128)(2,1)} %get-tuple-element.25) | copy-start | bytes 1572868
  57.9 1.2 %copy-start.2 = (bf16[256,1024]{1,0:T(8,128)(2,1)S(1)}, bf16[256,1024]{1,0:T(8,128)(2,1)}, u32[]{:S(2)}) copy-start(bf16[256,1024]{1,0:T(8,128)(2,1)} %get-tuple-element.26) | copy-start | bytes 1572868
  59.1 1.2 %copy-start.1 = (bf16[256,1024]{1,0:T(8,128)(2,1)S(1)}, bf16[256,1024]{1,0:T(8,128)(2,1)}, u32[]{:S(2)}) copy-start(bf16[256,1024]{1,0:T(8,128)(2,1)} %get-tuple-element.27) | copy-start | bytes 1572868
  60.3 1.2 %copy-start = (bf16[256,1024]{1,0:T(8,128)(2,1)S(1)}, bf16[256,1024]{1,0:T(8,128)(2,1)}, u32[]{:S(2)}) copy-start(bf16[256,1024]{1,0:T(8,128)(2,1)} %get-tuple-element.28) | copy-start | bytes 1572868
  61.6 0.8 %copy-start.4 = (f32[8,128]{1,0:T(8,128)S(1)}, f32[8,128]{1,0:T(8,128)}, u32[]{:S(2)}) copy-start(f32[8,128]{1,0:T(8,128)} %get-tuple-element.17) | copy-start | bytes 12292

commit v2 on v1

--- a/solution.py
+++ b/solution.py
@@ -13,6 +13,7 @@
 F32 = jnp.float32
 BF16 = jnp.bfloat16
 XS, CORES = 4, 2
+VIA_NEXT = 1
 
 
 def mm(a, b, ca, cb):
@@ -30,10 +31,10 @@
     xq, xk, xv, gl, og,
     ka, va, qa, qf, kl, vl, mg,
     wts, mix, ng, gng, sg, kp, vp, sk, sv,
-    lab, mask, acc, inv_b, cc_b,
-    own, sib_out, sib_in, tsend, tin, st,
+    gain8, lab, mask, acc, inv_b, cc_b,
+    own, sib_out, sib_in, tsend, tin, rx, st,
     meta, stat, gbuf,
-    in_sem, sib_s, sib_r, far_s, far_r, meta_s, meta_r, stat_s, stat_r, gain_s, gain_r,
+    in_sem, sib_s, sib_r, far_s, far_r, meta_s, meta_r, stat_s, stat_r, gain_s, gain_r, rel_s, rel_r, token,
 ):
     half = heads // 2
     features = heads * HD * n_head
@@ -46,13 +47,31 @@
     sibling = (g * 2 + 1 - p, y)
 
     def chip(d):
-        return (lax.rem(g + d + chips, chips) * 2 + p, y)
+        return ((g + d) * 2 + p, y)
+
+    def exists(chip_index):
+        return (chip_index >= 0) & (chip_index < chips)
+
+    def in_row(d):
+        return z * XS + lax.rem(x + d + XS, XS)
+
+    def at_z(other_z):
+        return ((other_z * XS + x) * 2 + p, y)
+
+    def when(cond, act):
+        pl.when(cond)(act)
 
     y_peers = [(c, lax.rem(y + d, n_head)) for d in range(1, n_head)]
-    x_peers = [((z * XS + lax.rem(x + d, XS)) * 2 + p, y) for d in range(1, XS)]
-    z_peers = [((lax.rem(z + d, zs) * XS + x) * 2 + p, y) for d in range(1, zs)]
-    near = [chip(1), chip(2), chip(-1), chip(-2)]
-    peers = [sibling] + near + y_peers + x_peers + z_peers
+    row_peers = [(in_row(d) * 2 + q, y) for d in range(1, XS) for q in (p, 1 - p)]
+    quad = min(zs, 4)
+    quad_peers = [at_z(z // quad * quad + lax.rem(z + d, quad)) for d in range(1, quad)]
+    far_z = lax.rem(z + quad, zs)
+    bridge = (z >= 2) & (z < 6)
+    near = [chip(k) for k in (1, 2, -1, -2)]
+    near_ok = [exists(g + k) for k in (1, 2, -1, -2)]
+    always = [sibling] + y_peers + row_peers[1::2] + quad_peers
+    chain = [(chip(k), exists(g + k)) for k in (1, 2, 3, -1, -2, -3)]
+    across = at_z(jnp.where(z < quad, z + 2, z - 2))
 
     loads = []
     for i, (src, dst) in enumerate(((xk_hbm, xk), (xv_hbm, xv), (xq_hbm, xq), (gl_hbm, gl), (og_hbm, og))):
@@ -60,8 +79,12 @@
         cp.start()
         loads.append(cp)
     barrier = pltpu.get_barrier_semaphore()
-    for q in peers:
+    greeted = jnp.int32(len(always))
+    for q in always:
         pl.semaphore_signal(barrier, inc=1, device_id=q, device_id_type=MESH)
+    for q, there in chain + ([(across, bridge)] if zs > quad else []):
+        when(there, lambda q=q: pl.semaphore_signal(barrier, inc=1, device_id=q, device_id_type=MESH))
+        greeted = greeted + there.astype(jnp.int32)
 
     def remote(src, dst, ssem, rsem, dev):
         return pltpu.make_async_remote_copy(
@@ -100,9 +123,34 @@
     def sib_copy(d, i, src):
         return remote(src, sib_in.at[d, i], sib_s.at[d, i], sib_r.at[d, i], sibling)
 
-    def far_copy(d, i, k):
-        step = (k + 1) * (1 if d == 0 else -1)
-        return remote(tsend.at[d, i], tin.at[d, k, i], far_s.at[d, k, i], far_r.at[d, k, i], chip(step))
+    def ok(d, k):
+        return exists(g + k * (1 - 2 * d))
+
+    def next_copy(d, i):
+        return remote(tsend.at[d, i], tin.at[d, 0, i], far_s.at[d, 0, i], far_r.at[d, 0, i], chip(1 - 2 * d))
+
+    def pass_copy(d, i):
+        return remote(tin.at[d, 0, i], tin.at[d, 1, i], far_s.at[d, 1, i], far_r.at[d, 1, i], chip(1 - 2 * d))
+
+    def back_copy(d, i):
+        return remote(tsend.at[d, i], rx.at[d, i], rel_s.at[d, i], rel_r.at[d, i], (in_row(2 * d - 1) * 2 + p, y))
+
+    def relay_target(d):
+        return in_row(1 - 2 * d) + 2 * (1 - 2 * d)
+
+    def relay_copy(d, i):
+        return remote(rx.at[d, i], tin.at[d, 1, i], far_s.at[d, 1, i], far_r.at[d, 1, i], (relay_target(d) * 2 + p, y))
+
+    def pass_on(d, i):
+        when(ok(d, -1), lambda: next_copy(d, i).wait_recv())
+        when(ok(d, -1) & ok(d, 1), lambda: pass_copy(d, i).start())
+
+    def relay(d, i):
+        def act():
+            back_copy(d, i).wait_recv()
+            relay_copy(d, i).start()
+
+        when(exists(relay_target(d)), act)
 
     def meta_copy(k):
         if k == 0:
@@ -114,7 +162,13 @@
     mine = p * half
     other = (1 - p) * half
     own_part(other)
-    pl.semaphore_wait(barrier, len(peers))
+    pl.semaphore_wait(barrier, greeted)
+    if zs > quad:
+        def tell():
+            for dz in (-2, 2):
+                pl.semaphore_signal(token, inc=1, device_id=at_z(z + dz), device_id_type=MESH)
+
+        when(bridge, tell)
     meta_copy(0).start()
     sib_copy(0, 0, own.at[other]).start()
 
@@ -134,7 +188,7 @@
     meta[2, 0:1, :] = f_lo
     meta[2, 1:2, :] = l_hi
     for k in range(1, 5):
-        meta_copy(k).start()
+        when(near_ok[k - 1], lambda k=k: meta_copy(k).start())
 
     def send_total(i, d):
         a, b = own[mine + i], sib_in[d, i]
@@ -144,8 +198,8 @@
         else:
             total = lo_part + jnp.where(f_lo == f_hi, hi_part, 0.0)
         tsend[d, i] = total
-        far_copy(d, i, 0).start()
-        far_copy(d, i, 1).start()
+        when(ok(d, 1), lambda: next_copy(d, i).start())
+        when(ok(d, 2) & (i >= VIA_NEXT), lambda: back_copy(d, i).start())
 
     def fwd_total(i):
         @pl.when(i > 0)
@@ -161,6 +215,7 @@
     s_iota = lax.broadcasted_iota(jnp.int32, (tokens, tokens), 1)
     lab2 = jnp.concatenate([lab[...]] * (tokens // HD), axis=1)
     mask[...] = jnp.where((lab2 == row) & (t_iota >= s_iota), 1.0, 0.0)
+    gain8[...] = gain_ref[...].astype(F32).reshape(heads, HD)
     loads[2].wait()
     loads[3].wait()
     loads[4].wait()
@@ -179,7 +234,7 @@
         sg[:, s] = gate
         grad = og[:, s].astype(F32) * gate
         ng[:, s] = grad
-        gng[:, s] = grad * gain_ref[:, s].astype(F32)
+        gng[:, s] = grad * gain8[pl.ds(h, 1), :]
         v = xv[:, s].astype(F32)
         gv = sigmoid(v)
         sv[:, s] = gv * (1.0 + v * (1.0 - gv))
@@ -189,25 +244,36 @@
         in_last = lab[...] == lab[tokens - 1 : tokens, :]
         vl[:, s] = jnp.where(in_last, va[:, s].astype(F32), 0.0).astype(BF16)
 
-    loop(heads, inside)
+    turns = [lambda i=i: pass_on(0, i) for i in range(VIA_NEXT)] + [lambda i=i: relay(0, i) for i in range(VIA_NEXT, half)]
+    split = heads - half // 2 - 1
+    loop(split, inside)
+    for j in range(half):
+        turns[j]()
+        if split + j < heads:
+            inside(split + j)
     acc[...] = jnp.zeros_like(acc)
 
-    for k in range(1, 5):
-        meta_copy(k).wait_recv()
+    for k, (back, slot) in enumerate(((2, 3), (3, 4), (0, 5), (1, 6))):
+        when(near_ok[back], lambda k=k: meta_copy(k + 1).wait_recv())
+
+        def missing(slot=slot):
+            meta[slot] = jnp.full(meta.shape[1:], -1.0, F32)
+
+        when(jnp.logical_not(near_ok[back]), missing)
 
     def receive(d, i, finish):
-        far_copy(d, i, 0).wait_recv()
-        far_copy(d, i, 1).wait_recv()
+        when(ok(d, -1) & (i >= VIA_NEXT), lambda: next_copy(d, i).wait_recv())
+        when(ok(d, -2), lambda: relay_copy(d, i).wait_recv())
         a, b = own[mine + i], sib_in[d, i]
         lo_part, hi_part = jnp.where(lo, a, b), jnp.where(lo, b, a)
         if d == 0:
-            near_ok, far_ok = meta[3, 1:2, :] == f_lo, meta[4, 1:2, :] == f_lo
-            edge = jnp.where(near_ok, tin[d, 0, i], 0.0) + jnp.where(far_ok, tin[d, 1, i], 0.0)
+            one, two = meta[3, 1:2, :] == f_lo, meta[4, 1:2, :] == f_lo
+            edge = jnp.where(one, tin[d, 0, i], 0.0) + jnp.where(two, tin[d, 1, i], 0.0)
             inner = jnp.where(l_lo == f_hi, lo_part, 0.0) + jnp.where(f_lo == f_hi, edge, 0.0)
             to_lo, to_hi = edge, inner
         else:
-            near_ok, far_ok = meta[5, 0:1, :] == l_hi, meta[6, 0:1, :] == l_hi
-            edge = jnp.where(near_ok, tin[d, 0, i], 0.0) + jnp.where(far_ok, tin[d, 1, i], 0.0)
+            one, two = meta[5, 0:1, :] == l_hi, meta[6, 0:1, :] == l_hi
+            edge = jnp.where(one, tin[d, 0, i], 0.0) + jnp.where(two, tin[d, 1, i], 0.0)
             inner = jnp.where(f_hi == l_lo, hi_part, 0.0) + jnp.where(l_hi == l_lo, edge, 0.0)
             to_lo, to_hi = inner, edge
         sib_out[d, i] = jnp.where(lo, to_hi, to_lo)
@@ -250,7 +316,10 @@
 
     def grad_part(h):
         s = cols(h)
-        m = (gng[:, s] * inv_b[...] - mix[:, s] * cc_b[...]).astype(BF16)
+        inv_r = inv_b[...]
+        plain = mix[:, s]
+        gbuf[0, pl.ds(h, 1), :] = jnp.sum(ng[:, s] * plain * inv_r, axis=0, keepdims=True)
+        m = (gng[:, s] * inv_r - plain * cc_b[...]).astype(BF16)
         mg[:, s] = m
         own[h] = mm(qf[:, s], m, 0, 0)
 
@@ -270,24 +339,39 @@
 
     loop(half, bwd_total)
 
+    def gain_copy(slot, dst, k, dev):
+        return remote(gbuf.at[slot], gbuf.at[dst], gain_s.at[k], gain_r.at[k], dev)
+
+    stages, k = [], 0
+    for partners in ([sibling] + row_peers, quad_peers, [at_z(far_z)] if zs > quad else []):
+        stages.append([gain_copy(len(stages), 4 + k + j, k + j, q) for j, q in enumerate(partners)])
+        k += len(partners)
+
+    def gain_stage(n):
+        total, first_slot = gbuf[n], 4 + sum(len(st_) for st_ in stages[:n])
+        for j, cp in enumerate(stages[n]):
+            cp.wait_recv()
+            total = total + gbuf[first_slot + j]
+        if n == 2:
+            gaing_ref[...] = total
+            return
+        gbuf[n + 1] = total
+        if n == 1 and zs > quad:
+            pl.semaphore_wait(token, 1)
+        for cp in stages[n + 1]:
+            cp.start()
+
+    for cp in stages[0]:
+        cp.start()
+
     def tail(h):
         s = cols(h)
-        unit = mix[:, s] * inv_b[...]
-        gbuf[0, pl.ds(h, 1), :] = jnp.sum(ng[:, s] * unit, axis=0, keepdims=True)
-        normed = unit * gain_ref[:, s].astype(F32)
+        normed = mix[:, s] * inv_b[...] * gain8[pl.ds(h, 1), :]
         gate = sg[:, s]
         attn_ref[:, s] = (normed * gate).astype(BF16)
         gg_ref[:, s] = (ng[:, s] * normed * (1.0 - gate)).astype(BF16)
 
     loop(heads, tail)
-
-    def gain_copy(slot, dst, k, dev):
-        return remote(gbuf.at[slot], gbuf.at[dst], gain_s.at[k], gain_r.at[k], dev)
-
-    core_copy = gain_copy(0, 3, 0, sibling)
-    x_copies = [gain_copy(1, 4 + k, 1 + k, q) for k, q in enumerate(x_peers)]
-    z_copies = [gain_copy(2, 4 + XS - 1 + k, XS + k, q) for k, q in enumerate(z_peers)]
-    core_copy.start()
 
     def pair(h):
         s = cols(h)
@@ -303,20 +387,15 @@
         part = mm(pg, ka[:, s], 1, 0) + jnp.where(in_first, mm(m, st[0, h], 1, 1), 0.0)
         qg_ref[:, s] = (part * slope).astype(BF16)
 
-    pair(0)
-    core_copy.wait_recv()
-    gbuf[1] = gbuf[0] + gbuf[3]
-    for cp in x_copies:
-        cp.start()
-    loop(half - 1, lambda i: pair(i + 1))
-    total = gbuf[1]
-    for k, cp in enumerate(x_copies):
-        cp.wait_recv()
-        total = total + gbuf[4 + k]
-    gbuf[2] = total
-    for cp in z_copies:
-        cp.start()
-    loop(half, lambda i: pair(half + i))
+    turns = [lambda i=i: pass_on(1, i) for i in range(VIA_NEXT)] + [lambda i=i: relay(1, i) for i in range(VIA_NEXT, half)]
+    loop(half, pair)
+    turns[0]()
+    gain_stage(0)
+    for j in range(1, half):
+        pair(half + j - 1)
+        turns[j]()
+    pair(heads - 1)
+    gain_stage(1)
 
     def final(h):
         s = cols(h)
@@ -325,28 +404,52 @@
         vg_ref[:, s] = ((vp[:, s] + mm(kl[:, s], gb, 1, 0)) * sv[:, s]).astype(BF16)
 
     loop(half, lambda i: receive(1, i, final))
-    total = gbuf[2]
-    for k, cp in enumerate(z_copies):
-        cp.wait_recv()
-        total = total + gbuf[4 + XS - 1 + k]
-    gaing_ref[...] = total
     loop(half, lambda i: receive_sib(1, i, final))
-
-    for k in range(5):
-        meta_copy(k).wait_send()
+    gain_stage(2)
+
+    meta_copy(0).wait_send()
+    for k in range(1, 5):
+        when(near_ok[k - 1], lambda k=k: meta_copy(k).wait_send())
     for k in range(n_head - 1):
         stat_copy(k).wait_send()
-    for cp in [core_copy] + x_copies + z_copies:
-        cp.wait_send()
+    for stage in stages:
+        for cp in stage:
+            cp.wait_send()
 
     def drain(i):
         sib_copy(1, i, own.at[other + i]).wait_send()
         for d in (0, 1):
             sib_copy(d, half + i, sib_out.at[d, i]).wait_send()
-            far_copy(d, i, 0).wait_send()
-            far_copy(d, i, 1).wait_send()
+            when(ok(d, 1), lambda d=d: next_copy(d, i).wait_send())
+            when(ok(d, 1) & ok(d, -1) & (i < VIA_NEXT), lambda d=d: pass_copy(d, i).wait_send())
+
+            def relayed(d=d):
+                relay_copy(d, i).wait_send()
+
+            when(ok(d, 2) & (i >= VIA_NEXT), lambda d=d: back_copy(d, i).wait_send())
+            when(exists(relay_target(d)) & (i >= VIA_NEXT), relayed)
 
     loop(half, drain)
+
+
+def write_kernel(n, *refs):
+    sems = refs[-1]
+    copies = [pltpu.make_async_copy(refs[i], refs[n + i], sems.at[i]) for i in range(n)]
+    for cp in copies:
+        cp.start()
+    for cp in copies:
+        cp.wait()
+
+
+def write_out(arrays):
+    n = len(arrays)
+    return pl.pallas_call(
+        functools.partial(write_kernel, n),
+        out_shape=tuple(jax.ShapeDtypeStruct(a.shape, a.dtype) for a in arrays),
+        in_specs=[pl.BlockSpec(memory_space=pltpu.VMEM)] * n,
+        out_specs=(pl.BlockSpec(memory_space=pl.ANY),) * n,
+        scratch_shapes=[pltpu.SemaphoreType.DMA((n,))],
+    )(*arrays)
 
 
 def local(n_ctx, n_head, x_query, x_key, x_value, gate_logits, norm_gain, out_grad, doc_ids):
@@ -360,32 +463,34 @@
     thin = pltpu.VMEM((tokens, HD), F32)
     state = lambda *lead: pltpu.VMEM((*lead, HD, HD), F32)
     dma = pltpu.SemaphoreType.DMA
-    n_gain = 1 + (XS - 1) + (zs - 1)
+    n_gain = 1 + 2 * (XS - 1) + min(zs, 4)
     vmem = pl.BlockSpec(memory_space=pltpu.VMEM)
     anywhere = pl.BlockSpec(memory_space=pl.ANY)
-    big = jax.ShapeDtypeStruct((tokens, width), BF16)
+    big = pltpu.VMEM((tokens, width), BF16)
     outs = pl.pallas_call(
         functools.partial(kernel, n_ctx, n_head, heads),
-        out_shape=(big, big, big, big, big, jax.ShapeDtypeStruct((heads, HD), F32)),
+        out_shape=(big, big, big, big, big, pltpu.VMEM((heads, HD), F32)),
         in_specs=[anywhere] * 5 + [vmem] * 2,
         out_specs=(vmem,) * 6,
         scratch_shapes=[flat16] * 5 + [flat16] * 7
         + [pltpu.VMEM((heads, tokens, tokens), BF16)] + [flat32] * 8
-        + [thin, square, pltpu.VMEM((2, tokens, HD), F32), thin, thin]
+        + [pltpu.VMEM((heads, HD), F32), thin, square, pltpu.VMEM((2, tokens, HD), F32), thin, thin]
         + [
-            state(heads), state(2, half), state(2, 2 * half), state(2, half), state(2, 2, half),
+            state(heads), state(2, half), state(2, 2 * half), state(2, half), state(2, 2, half), state(2, half),
             pltpu.VMEM((2, heads, HD, HD), BF16),
             pltpu.VMEM((7, 8, HD), F32),
             pltpu.VMEM((n_head, 8, tokens), F32),
-            pltpu.VMEM((3 + n_gain, heads, HD), F32),
+            pltpu.VMEM((4 + n_gain, heads, HD), F32),
             dma((5,)), dma((2, 2 * half)), dma((2, 2 * half)), dma((2, 2, half)), dma((2, 2, half)),
             dma((5,)), dma((5,)), dma((n_head - 1,)), dma((n_head - 1,)), dma((n_gain,)), dma((n_gain,)),
+            dma((2, half)), dma((2, half)), pltpu.SemaphoreType.REGULAR,
         ],
         compiler_params=pltpu.CompilerParams(
             collective_id=0, has_side_effects=True, vmem_limit_bytes=56 << 20
         ),
         cost_estimate=pl.CostEstimate(flops=1 << 30, bytes_accessed=5 << 20, transcendentals=1 << 20),
-    )(x_query, x_key, x_value, gate_logits, out_grad, norm_gain.reshape(1, width), doc_ids.reshape(1, tokens))
+    )(x_query, x_key, x_value, gate_logits, out_grad, norm_gain, doc_ids.reshape(1, tokens))
+    outs = write_out([pltpu.with_memory_space_constraint(a, pltpu.VMEM) for a in outs])
     return (*outs[:5], outs[5].reshape(width))
 
 

time: 64 us -> 50.9 us (0.80)
  the two profiles are of different devices: /device:TPU:1 before, /device:TPU:34 now
where the time goes in v2:
time: 50.9 us; the launch traced here: 50.8 us
  Pallas kernels  50.1 us (98%)
  between operations  0.64 us (1%)
    pallas_call x1, Pallas kernels, local(): pl.pallas_call(functools.partial(kernel, n_ctx, n_head, heads), out_shape...  48.6 us
    pallas_call x1, Pallas kernels, write_out(): pl.pallas_call(functools.partial(write_kernel, n), out_shape=tuple((jax.S...  1.54 us

profile of v2, /device:TPU:34, one launch (start us, length us, event | category | flops | bytes accessed | tf_op | source)
XLA Modules:
  0.0 50.8 jit_solution(7356887398812219092)
XLA Ops:
  0.6 48.6 %shard_map.118 = (bf16[256,1024]{1,0:T(8,128)(2,1)S(1)}, bf16[256,1024]{1,0:T(8,128)(2,1)S(1)}, bf16[256,1024]{1,0:T(8,128)(2,1)S(1)}, bf16[256,1024]{1,0:T(8,12...) custom-call(bf16[256,1024]{1,0:T(8,128)(2,1)} %xq_hbm.1, bf16[256,1024]{1,0:T(8,128)(2,1)} %xk_hbm.1, ...), custom_call_target="tpu_custom_call" | custom-call | flops 1073741824 | bytes 5242880 | tf_op jit(solution)/shard_map/pallas_call | solution.py:470
  49.2 1.5 %shard_map.119 = (bf16[256,1024]{1,0:T(8,128)(2,1)}, bf16[256,1024]{1,0:T(8,128)(2,1)}, bf16[256,1024]{1,0:T(8,128)(2,1)}, bf16[256,1024]{1,0:T(8,128)(2,1)}, bf...) custom-call(bf16[256,1024]{1,0:T(8,128)(2,1)S(1)} %get-tuple-element.18.refs_0_, ...), custom_call_target="tpu_custom_call" | custom-call | tf_op jit(solution)/shard_map/pallas_call | solution.py:446

commit v3 on v2

--- a/solution.py
+++ b/solution.py
@@ -13,7 +13,7 @@
 F32 = jnp.float32
 BF16 = jnp.bfloat16
 XS, CORES = 4, 2
-VIA_NEXT = 1
+VIA_NEXT = 2
 
 
 def mm(a, b, ca, cb):
@@ -65,13 +65,13 @@
     row_peers = [(in_row(d) * 2 + q, y) for d in range(1, XS) for q in (p, 1 - p)]
     quad = min(zs, 4)
     quad_peers = [at_z(z // quad * quad + lax.rem(z + d, quad)) for d in range(1, quad)]
-    far_z = lax.rem(z + quad, zs)
-    bridge = (z >= 2) & (z < 6)
+    z_peers = [at_z(lax.rem(z + d, zs)) for d in range(1, zs)]
+    lead = (z == 2) | (z == 4)
     near = [chip(k) for k in (1, 2, -1, -2)]
     near_ok = [exists(g + k) for k in (1, 2, -1, -2)]
     always = [sibling] + y_peers + row_peers[1::2] + quad_peers
     chain = [(chip(k), exists(g + k)) for k in (1, 2, 3, -1, -2, -3)]
-    across = at_z(jnp.where(z < quad, z + 2, z - 2))
+    across = at_z(jnp.where(z < quad, 4, 2))
 
     loads = []
     for i, (src, dst) in enumerate(((xk_hbm, xk), (xv_hbm, xv), (xq_hbm, xq), (gl_hbm, gl), (og_hbm, og))):
@@ -82,7 +82,7 @@
     greeted = jnp.int32(len(always))
     for q in always:
         pl.semaphore_signal(barrier, inc=1, device_id=q, device_id_type=MESH)
-    for q, there in chain + ([(across, bridge)] if zs > quad else []):
+    for q, there in chain + ([(across, lead)] if zs > quad else []):
         when(there, lambda q=q: pl.semaphore_signal(barrier, inc=1, device_id=q, device_id_type=MESH))
         greeted = greeted + there.astype(jnp.int32)
 
@@ -164,11 +164,7 @@
     own_part(other)
     pl.semaphore_wait(barrier, greeted)
     if zs > quad:
-        def tell():
-            for dz in (-2, 2):
-                pl.semaphore_signal(token, inc=1, device_id=at_z(z + dz), device_id_type=MESH)
-
-        when(bridge, tell)
+        when(lead, lambda: pl.semaphore_signal(token, inc=1, device_id=across, device_id_type=MESH))
     meta_copy(0).start()
     sib_copy(0, 0, own.at[other]).start()
 
@@ -210,6 +206,14 @@
         send_total(i, 0)
 
     loop(half, fwd_total)
+
+    if zs > quad:
+        def spread():
+            pl.semaphore_wait(token, 1)
+            for q in quad_peers:
+                pl.semaphore_signal(token, inc=1, device_id=q, device_id_type=MESH)
+
+        when(lead, spread)
 
     t_iota = lax.broadcasted_iota(jnp.int32, (tokens, tokens), 0)
     s_iota = lax.broadcasted_iota(jnp.int32, (tokens, tokens), 1)
@@ -314,12 +318,39 @@
     inv_b[...] = jnp.broadcast_to(inv, (HD, tokens)).T
     cc_b[...] = jnp.broadcast_to(cc, (HD, tokens)).T
 
+    def gain_copy(slot, dst, k, dev):
+        return remote(gbuf.at[slot], gbuf.at[dst], gain_s.at[k], gain_r.at[k], dev)
+
+    stages, k = [], 0
+    for partners in ([sibling] + row_peers, z_peers):
+        stages.append([gain_copy(len(stages), 2 + k + j, k + j, q) for j, q in enumerate(partners)])
+        k += len(partners)
+
+    def gain_stage(n):
+        total, first_slot = gbuf[n], 2 + sum(len(st_) for st_ in stages[:n])
+        for j, cp in enumerate(stages[n]):
+            cp.wait_recv()
+            total = total + gbuf[first_slot + j]
+        if n == 1:
+            gaing_ref[...] = total
+            return
+        gbuf[n + 1] = total
+        if zs > quad:
+            when(jnp.logical_not(lead), lambda: pl.semaphore_wait(token, 1))
+        for cp in stages[n + 1]:
+            cp.start()
+
+    def gain_row(h):
+        s = cols(h)
+        gbuf[0, pl.ds(h, 1), :] = jnp.sum(ng[:, s] * mix[:, s] * inv_b[...], axis=0, keepdims=True)
+
+    loop(heads, gain_row)
+    for cp in stages[0]:
+        cp.start()
+
     def grad_part(h):
         s = cols(h)
-        inv_r = inv_b[...]
-        plain = mix[:, s]
-        gbuf[0, pl.ds(h, 1), :] = jnp.sum(ng[:, s] * plain * inv_r, axis=0, keepdims=True)
-        m = (gng[:, s] * inv_r - plain * cc_b[...]).astype(BF16)
+        m = (gng[:, s] * inv_b[...] - mix[:, s] * cc_b[...]).astype(BF16)
         mg[:, s] = m
         own[h] = mm(qf[:, s], m, 0, 0)
 
@@ -338,31 +369,6 @@
         send_total(i, 1)
 
     loop(half, bwd_total)
-
-    def gain_copy(slot, dst, k, dev):
-        return remote(gbuf.at[slot], gbuf.at[dst], gain_s.at[k], gain_r.at[k], dev)
-
-    stages, k = [], 0
-    for partners in ([sibling] + row_peers, quad_peers, [at_z(far_z)] if zs > quad else []):
-        stages.append([gain_copy(len(stages), 4 + k + j, k + j, q) for j, q in enumerate(partners)])
-        k += len(partners)
-
-    def gain_stage(n):
-        total, first_slot = gbuf[n], 4 + sum(len(st_) for st_ in stages[:n])
-        for j, cp in enumerate(stages[n]):
-            cp.wait_recv()
-            total = total + gbuf[first_slot + j]
-        if n == 2:
-            gaing_ref[...] = total
-            return
-        gbuf[n + 1] = total
-        if n == 1 and zs > quad:
-            pl.semaphore_wait(token, 1)
-        for cp in stages[n + 1]:
-            cp.start()
-
-    for cp in stages[0]:
-        cp.start()
 
     def tail(h):
         s = cols(h)
@@ -387,15 +393,15 @@
         part = mm(pg, ka[:, s], 1, 0) + jnp.where(in_first, mm(m, st[0, h], 1, 1), 0.0)
         qg_ref[:, s] = (part * slope).astype(BF16)
 
-    turns = [lambda i=i: pass_on(1, i) for i in range(VIA_NEXT)] + [lambda i=i: relay(1, i) for i in range(VIA_NEXT, half)]
-    loop(half, pair)
+    turns = [lambda i=i: relay(1, i) for i in range(VIA_NEXT, half)] + [lambda i=i: pass_on(1, i) for i in range(VIA_NEXT)]
+    loop(2, pair)
+    gain_stage(0)
+    loop(half - 2, lambda i: pair(2 + i))
     turns[0]()
-    gain_stage(0)
     for j in range(1, half):
         pair(half + j - 1)
         turns[j]()
     pair(heads - 1)
-    gain_stage(1)
 
     def final(h):
         s = cols(h)
@@ -405,7 +411,7 @@
 
     loop(half, lambda i: receive(1, i, final))
     loop(half, lambda i: receive_sib(1, i, final))
-    gain_stage(2)
+    gain_stage(1)
 
     meta_copy(0).wait_send()
     for k in range(1, 5):
@@ -463,7 +469,7 @@
     thin = pltpu.VMEM((tokens, HD), F32)
     state = lambda *lead: pltpu.VMEM((*lead, HD, HD), F32)
     dma = pltpu.SemaphoreType.DMA
-    n_gain = 1 + 2 * (XS - 1) + min(zs, 4)
+    n_gain = 1 + 2 * (XS - 1) + zs - 1
     vmem = pl.BlockSpec(memory_space=pltpu.VMEM)
     anywhere = pl.BlockSpec(memory_space=pl.ANY)
     big = pltpu.VMEM((tokens, width), BF16)
@@ -480,7 +486,7 @@
             pltpu.VMEM((2, heads, HD, HD), BF16),
             pltpu.VMEM((7, 8, HD), F32),
             pltpu.VMEM((n_head, 8, tokens), F32),
-            pltpu.VMEM((4 + n_gain, heads, HD), F32),
+            pltpu.VMEM((2 + n_gain, heads, HD), F32),
             dma((5,)), dma((2, 2 * half)), dma((2, 2 * half)), dma((2, 2, half)), dma((2, 2, half)),
             dma((5,)), dma((5,)), dma((n_head - 1,)), dma((n_head - 1,)), dma((n_gain,)), dma((n_gain,)),
             dma((2, half)), dma((2, half)), pltpu.SemaphoreType.REGULAR,

time: 50.9 us -> 45.1 us (0.89)
  the two profiles are of different devices: /device:TPU:34 before, /device:TPU:103 now
where the time goes in v3:
time: 45.1 us; the launch traced here: 44.9 us
  Pallas kernels  44.3 us (98%)
  between operations  0.64 us (1%)
    pallas_call x1, Pallas kernels, local(): pl.pallas_call(functools.partial(kernel, n_ctx, n_head, heads), out_shape...  42.7 us
    pallas_call x1, Pallas kernels, write_out(): pl.pallas_call(functools.partial(write_kernel, n), out_shape=tuple((jax.S...  1.54 us

profile of v3, /device:TPU:103, one launch (start us, length us, event | category | flops | bytes accessed | tf_op | source)
XLA Modules:
  0.0 44.9 jit_solution(16088285787114393602)
XLA Ops:
  0.6 42.7 %shard_map.118 = (bf16[256,1024]{1,0:T(8,128)(2,1)S(1)}, bf16[256,1024]{1,0:T(8,128)(2,1)S(1)}, bf16[256,1024]{1,0:T(8,128)(2,1)S(1)}, bf16[256,1024]{1,0:T(8,12...) custom-call(bf16[256,1024]{1,0:T(8,128)(2,1)} %xq_hbm.1, bf16[256,1024]{1,0:T(8,128)(2,1)} %xk_hbm.1, ...), custom_call_target="tpu_custom_call" | custom-call | flops 1073741824 | bytes 5242880 | tf_op jit(solution)/shard_map/pallas_call | solution.py:476
  43.4 1.5 %shard_map.119 = (bf16[256,1024]{1,0:T(8,128)(2,1)}, bf16[256,1024]{1,0:T(8,128)(2,1)}, bf16[256,1024]{1,0:T(8,128)(2,1)}, bf16[256,1024]{1,0:T(8,128)(2,1)}, bf...) custom-call(bf16[256,1024]{1,0:T(8,128)(2,1)S(1)} %get-tuple-element.18.refs_0_, ...), custom_call_target="tpu_custom_call" | custom-call | tf_op jit(solution)/shard_map/pallas_call | solution.py:452

commit v4 on v3

--- a/solution.py
+++ b/solution.py
@@ -13,7 +13,7 @@
 F32 = jnp.float32
 BF16 = jnp.bfloat16
 XS, CORES = 4, 2
-VIA_NEXT = 2
+VIA_NEXT = 1
 
 
 def mm(a, b, ca, cb):
@@ -26,12 +26,12 @@
 
 def kernel(
     n_ctx, n_head, heads,
-    xq_hbm, xk_hbm, xv_hbm, gl_hbm, og_hbm, gain_ref, doc_ref,
+    xq_hbm, xk_hbm, xv_hbm, gl_hbm, og_hbm, gain_hbm, doc_hbm,
     attn_ref, qg_ref, kg_ref, vg_ref, gg_ref, gaing_ref,
     xq, xk, xv, gl, og,
     ka, va, qa, qf, kl, vl, mg,
     wts, mix, ng, gng, sg, kp, vp, sk, sv,
-    gain8, lab, mask, acc, inv_b, cc_b,
+    gain16, docs, gain8, lab, mask, acc, inv_b, cc_b,
     own, sib_out, sib_in, tsend, tin, rx, st,
     meta, stat, gbuf,
     in_sem, sib_s, sib_r, far_s, far_r, meta_s, meta_r, stat_s, stat_r, gain_s, gain_r, rel_s, rel_r, token,
@@ -74,7 +74,9 @@
     across = at_z(jnp.where(z < quad, 4, 2))
 
     loads = []
-    for i, (src, dst) in enumerate(((xk_hbm, xk), (xv_hbm, xv), (xq_hbm, xq), (gl_hbm, gl), (og_hbm, og))):
+    for i, (src, dst) in enumerate(
+        ((doc_hbm, docs), (xk_hbm, xk), (xv_hbm, xv), (xq_hbm, xq), (gl_hbm, gl), (og_hbm, og), (gain_hbm, gain16))
+    ):
         cp = pltpu.make_async_copy(src, dst, in_sem.at[i])
         cp.start()
         loads.append(cp)
@@ -97,7 +99,8 @@
     def cols(h):
         return pl.ds(pl.multiple_of(h * HD, HD), HD)
 
-    row = doc_ref[...].astype(F32)
+    loads[0].wait()
+    row = docs[...].astype(F32)
     tokens = row.shape[1]
     lab[...] = jnp.broadcast_to(row, (HD, tokens)).T
     first, last = lab[0:1, :], lab[tokens - 1 : tokens, :]
@@ -107,18 +110,21 @@
     meta[0, 0:1, :] = first
     meta[0, 1:2, :] = last
 
-    def own_part(h):
-        s = cols(h)
-        k = xk[:, s].astype(F32)
-        v = xv[:, s].astype(F32)
-        kb = (k * sigmoid(k)).astype(BF16)
-        vb = (v * sigmoid(v)).astype(BF16)
-        ka[:, s] = kb
-        va[:, s] = vb
+    def own_part(*which):
+        raw = [(xk[:, cols(h)].astype(F32), xv[:, cols(h)].astype(F32)) for h in which]
         in_last = lab[...] == lab[tokens - 1 : tokens, :]
-        kb = jnp.where(in_last, kb.astype(F32), 0.0).astype(BF16)
-        kl[:, s] = kb
-        own[h] = mm(kb, vb, 0, 0)
+        done = []
+        for k, v in raw:
+            kb = (k * sigmoid(k)).astype(BF16)
+            vb = (v * sigmoid(v)).astype(BF16)
+            kept = jnp.where(in_last, kb.astype(F32), 0.0).astype(BF16)
+            done.append((kb, vb, kept, mm(kept, vb, 0, 0)))
+        for h, (kb, vb, kept, part) in zip(which, done):
+            s = cols(h)
+            ka[:, s] = kb
+            va[:, s] = vb
+            kl[:, s] = kept
+            own[h] = part
 
     def sib_copy(d, i, src):
         return remote(src, sib_in.at[d, i], sib_s.at[d, i], sib_r.at[d, i], sibling)
@@ -133,10 +139,17 @@
         return remote(tin.at[d, 0, i], tin.at[d, 1, i], far_s.at[d, 1, i], far_r.at[d, 1, i], chip(1 - 2 * d))
 
     def back_copy(d, i):
-        return remote(tsend.at[d, i], rx.at[d, i], rel_s.at[d, i], rel_r.at[d, i], (in_row(2 * d - 1) * 2 + p, y))
+        return remote(tsend.at[d, i], rx.at[d, i], rel_s.at[d, i], rel_r.at[d, i], (relay_of(d) * 2 + p, y))
+
+    def relay_of(d):
+        return jnp.where(x == 2 - d, g + 3 * (1 - 2 * d), in_row(2 * d - 1))
 
     def relay_target(d):
-        return in_row(1 - 2 * d) + 2 * (1 - 2 * d)
+        return jnp.where(x == 1 + d, g - 3 * (1 - 2 * d), in_row(1 - 2 * d)) + 2 * (1 - 2 * d)
+
+    def relay_ok(d):
+        source = relay_target(d) - 2 * (1 - 2 * d)
+        return exists(relay_target(d)) & exists(source)
 
     def relay_copy(d, i):
         return remote(rx.at[d, i], tin.at[d, 1, i], far_s.at[d, 1, i], far_r.at[d, 1, i], (relay_target(d) * 2 + p, y))
@@ -150,15 +163,22 @@
             back_copy(d, i).wait_recv()
             relay_copy(d, i).start()
 
-        when(exists(relay_target(d)), act)
+        when(relay_ok(d), act)
+
+    def turn(d, j):
+        first = [lambda i=i: pass_on(d, i) for i in range(VIA_NEXT)]
+        then = [lambda i=i: relay(d, i) for i in range(VIA_NEXT, half)]
+        edge = x == d * (XS - 1)
+        when(edge, (then + first)[j])
+        when(jnp.logical_not(edge), (first + then)[j])
 
     def meta_copy(k):
         if k == 0:
             return remote(meta.at[0], meta.at[1], meta_s.at[0], meta_r.at[0], sibling)
         return remote(meta.at[2], meta.at[2 + k], meta_s.at[k], meta_r.at[k], near[k - 1])
 
-    loads[0].wait()
     loads[1].wait()
+    loads[2].wait()
     mine = p * half
     other = (1 - p) * half
     own_part(other)
@@ -168,11 +188,16 @@
     meta_copy(0).start()
     sib_copy(0, 0, own.at[other]).start()
 
-    def send_own(i):
-        own_part(other + i + 1)
+    def send_own(j):
+        i = 2 * j + 1
+        own_part(other + i, other + i + 1)
+        sib_copy(0, i, own.at[other + i]).start()
         sib_copy(0, i + 1, own.at[other + i + 1]).start()
 
-    loop(half - 1, send_own)
+    loop((half - 1) // 2, send_own)
+    if half % 2 == 0:
+        own_part(other + half - 1)
+        sib_copy(0, half - 1, own.at[other + half - 1]).start()
 
     own_part(mine)
     meta_copy(0).wait_recv()
@@ -198,14 +223,20 @@
         when(ok(d, 2) & (i >= VIA_NEXT), lambda: back_copy(d, i).start())
 
     def fwd_total(i):
-        @pl.when(i > 0)
-        def _():
-            own_part(mine + i)
-
         sib_copy(0, i, own.at[other + i]).wait_recv()
         send_total(i, 0)
 
-    loop(half, fwd_total)
+    fwd_total(0)
+
+    def fwd_totals(j):
+        own_part(mine + 2 * j + 1, mine + 2 * j + 2)
+        fwd_total(2 * j + 1)
+        fwd_total(2 * j + 2)
+
+    loop((half - 1) // 2, fwd_totals)
+    if half % 2 == 0:
+        own_part(mine + half - 1)
+        fwd_total(half - 1)
 
     if zs > quad:
         def spread():
@@ -219,10 +250,9 @@
     s_iota = lax.broadcasted_iota(jnp.int32, (tokens, tokens), 1)
     lab2 = jnp.concatenate([lab[...]] * (tokens // HD), axis=1)
     mask[...] = jnp.where((lab2 == row) & (t_iota >= s_iota), 1.0, 0.0)
-    gain8[...] = gain_ref[...].astype(F32).reshape(heads, HD)
-    loads[2].wait()
-    loads[3].wait()
-    loads[4].wait()
+    for load in loads[3:]:
+        load.wait()
+    gain8[...] = gain16[...].astype(F32).reshape(heads, HD)
 
     def inside(h):
         s = cols(h)
@@ -248,11 +278,10 @@
         in_last = lab[...] == lab[tokens - 1 : tokens, :]
         vl[:, s] = jnp.where(in_last, va[:, s].astype(F32), 0.0).astype(BF16)
 
-    turns = [lambda i=i: pass_on(0, i) for i in range(VIA_NEXT)] + [lambda i=i: relay(0, i) for i in range(VIA_NEXT, half)]
     split = heads - half // 2 - 1
     loop(split, inside)
     for j in range(half):
-        turns[j]()
+        turn(0, j)
         if split + j < heads:
             inside(split + j)
     acc[...] = jnp.zeros_like(acc)
@@ -348,27 +377,34 @@
     for cp in stages[0]:
         cp.start()
 
-    def grad_part(h):
-        s = cols(h)
-        m = (gng[:, s] * inv_b[...] - mix[:, s] * cc_b[...]).astype(BF16)
-        mg[:, s] = m
-        own[h] = mm(qf[:, s], m, 0, 0)
+    def grad_part(*which):
+        inv_r, cc_r = inv_b[...], cc_b[...]
+        raw = [(gng[:, cols(h)], mix[:, cols(h)], qf[:, cols(h)]) for h in which]
+        done = []
+        for grad, plain, queries in raw:
+            m = (grad * inv_r - plain * cc_r).astype(BF16)
+            done.append((m, mm(queries, m, 0, 0)))
+        for h, (m, part) in zip(which, done):
+            mg[:, cols(h)] = m
+            own[h] = part
 
     for i in range(half):
         sib_copy(0, i, own.at[other + i]).wait_send()
 
-    def send_grad(i):
-        grad_part(other + i)
-        sib_copy(1, i, own.at[other + i]).start()
-
-    loop(half, send_grad)
-
-    def bwd_total(i):
-        grad_part(mine + i)
-        sib_copy(1, i, own.at[other + i]).wait_recv()
-        send_total(i, 1)
-
-    loop(half, bwd_total)
+    def send_grad(j):
+        grad_part(other + 2 * j, other + 2 * j + 1)
+        for i in (2 * j, 2 * j + 1):
+            sib_copy(1, i, own.at[other + i]).start()
+
+    loop(half // 2, send_grad)
+
+    def bwd_total(j):
+        grad_part(mine + 2 * j, mine + 2 * j + 1)
+        for i in (2 * j, 2 * j + 1):
+            sib_copy(1, i, own.at[other + i]).wait_recv()
+            send_total(i, 1)
+
+    loop(half // 2, bwd_total)
 
     def tail(h):
         s = cols(h)
@@ -393,14 +429,13 @@
         part = mm(pg, ka[:, s], 1, 0) + jnp.where(in_first, mm(m, st[0, h], 1, 1), 0.0)
         qg_ref[:, s] = (part * slope).astype(BF16)
 
-    turns = [lambda i=i: relay(1, i) for i in range(VIA_NEXT, half)] + [lambda i=i: pass_on(1, i) for i in range(VIA_NEXT)]
     loop(2, pair)
     gain_stage(0)
     loop(half - 2, lambda i: pair(2 + i))
-    turns[0]()
+    turn(1, 0)
     for j in range(1, half):
         pair(half + j - 1)
-        turns[j]()
+        turn(1, j)
     pair(heads - 1)
 
     def final(h):
@@ -433,7 +468,7 @@
                 relay_copy(d, i).wait_send()
 
             when(ok(d, 2) & (i >= VIA_NEXT), lambda d=d: back_copy(d, i).wait_send())
-            when(exists(relay_target(d)) & (i >= VIA_NEXT), relayed)
+            when(relay_ok(d) & (i >= VIA_NEXT), relayed)
 
     loop(half, drain)
 
@@ -476,18 +511,18 @@
     outs = pl.pallas_call(
         functools.partial(kernel, n_ctx, n_head, heads),
         out_shape=(big, big, big, big, big, pltpu.VMEM((heads, HD), F32)),
-        in_specs=[anywhere] * 5 + [vmem] * 2,
+        in_specs=[anywhere] * 7,
         out_specs=(vmem,) * 6,
         scratch_shapes=[flat16] * 5 + [flat16] * 7
         + [pltpu.VMEM((heads, tokens, tokens), BF16)] + [flat32] * 8
-        + [pltpu.VMEM((heads, HD), F32), thin, square, pltpu.VMEM((2, tokens, HD), F32), thin, thin]
+        + [pltpu.VMEM((width,), BF16), pltpu.VMEM((1, tokens), jnp.int32), pltpu.VMEM((heads, HD), F32), thin, square, pltpu.VMEM((2, tokens, HD), F32), thin, thin]
         + [
             state(heads), state(2, half), state(2, 2 * half), state(2, half), state(2, 2, half), state(2, half),
             pltpu.VMEM((2, heads, HD, HD), BF16),
             pltpu.VMEM((7, 8, HD), F32),
             pltpu.VMEM((n_head, 8, tokens), F32),
             pltpu.VMEM((2 + n_gain, heads, HD), F32),
-            dma((5,)), dma((2, 2 * half)), dma((2, 2 * half)), dma((2, 2, half)), dma((2, 2, half)),
+            dma((7,)), dma((2, 2 * half)), dma((2, 2 * half)), dma((2, 2, half)), dma((2, 2, half)),
             dma((5,)), dma((5,)), dma((n_head - 1,)), dma((n_head - 1,)), dma((n_gain,)), dma((n_gain,)),
             dma((2, half)), dma((2, half)), pltpu.SemaphoreType.REGULAR,
         ],

time: 45.1 us -> 43 us (0.953)
  the two profiles are of different devices: /device:TPU:103 before, /device:TPU:1 now
where the time goes in v4:
time: 43 us; the launch traced here: 42.9 us
  Pallas kernels  42.2 us (98%)
  between operations  0.64 us (1%)
    pallas_call x1, Pallas kernels, local(): pl.pallas_call(functools.partial(kernel, n_ctx, n_head, heads), out_shape...  40.7 us
    pallas_call x1, Pallas kernels, write_out(): pl.pallas_call(functools.partial(write_kernel, n), out_shape=tuple((jax.S...  1.54 us

profile of v4, /device:TPU:1, one launch (start us, length us, event | category | flops | bytes accessed | tf_op | source)
XLA Modules:
  0.0 42.9 jit_solution(9373590531745439570)
XLA Ops:
  0.6 40.7 %shard_map.118 = (bf16[256,1024]{1,0:T(8,128)(2,1)S(1)}, bf16[256,1024]{1,0:T(8,128)(2,1)S(1)}, bf16[256,1024]{1,0:T(8,128)(2,1)S(1)}, bf16[256,1024]{1,0:T(8,12...) custom-call(bf16[256,1024]{1,0:T(8,128)(2,1)} %xq_hbm.1, bf16[256,1024]{1,0:T(8,128)(2,1)} %xk_hbm.1, ...), custom_call_target="tpu_custom_call" | custom-call | flops 1073741824 | bytes 5242880 | tf_op jit(solution)/shard_map/pallas_call | solution.py:511
  41.3 1.5 %shard_map.119 = (bf16[256,1024]{1,0:T(8,128)(2,1)}, bf16[256,1024]{1,0:T(8,128)(2,1)}, bf16[256,1024]{1,0:T(8,128)(2,1)}, bf16[256,1024]{1,0:T(8,128)(2,1)}, bf...) custom-call(bf16[256,1024]{1,0:T(8,128)(2,1)S(1)} %get-tuple-element.18.refs_0_, ...), custom_call_target="tpu_custom_call" | custom-call | tf_op jit(solution)/shard_map/pallas_call | solution.py:487

commit v5 on v4

--- a/solution.py
+++ b/solution.py
@@ -13,7 +13,9 @@
 F32 = jnp.float32
 BF16 = jnp.bfloat16
 XS, CORES = 4, 2
-VIA_NEXT = 1
+PIECES = 2
+VIA_NEXT = 3
+VIA_ROW = 1
 
 
 def mm(a, b, ca, cb):
@@ -37,6 +39,8 @@
     in_sem, sib_s, sib_r, far_s, far_r, meta_s, meta_r, stat_s, stat_r, gain_s, gain_r, rel_s, rel_r, token,
 ):
     half = heads // 2
+    depth = HD // PIECES
+    pieces = half * PIECES
     features = heads * HD * n_head
     c, y = lax.axis_index("ctx"), lax.axis_index("head")
     p = lax.rem(c, 2)
@@ -154,23 +158,43 @@
     def relay_copy(d, i):
         return remote(rx.at[d, i], tin.at[d, 1, i], far_s.at[d, 1, i], far_r.at[d, 1, i], (relay_target(d) * 2 + p, y))
 
+    def via(here):
+        return jnp.where(here, VIA_ROW, VIA_NEXT)
+
+    def passed(d, j):
+        return j < via(x == (1 - d) * (XS - 1))
+
+    def sent_back(d, j):
+        return j >= via(x == 2 - d)
+
+    def relayed(d, j):
+        return j >= via(x == 1 + d)
+
     def pass_on(d, i):
-        when(ok(d, -1), lambda: next_copy(d, i).wait_recv())
-        when(ok(d, -1) & ok(d, 1), lambda: pass_copy(d, i).start())
+        when(ok(d, -1) & passed(d, i), lambda: next_copy(d, i).wait_recv())
+        when(ok(d, -1) & ok(d, 1) & passed(d, i), lambda: pass_copy(d, i).start())
 
     def relay(d, i):
         def act():
             back_copy(d, i).wait_recv()
             relay_copy(d, i).start()
 
-        when(relay_ok(d), act)
-
-    def turn(d, j):
-        first = [lambda i=i: pass_on(d, i) for i in range(VIA_NEXT)]
-        then = [lambda i=i: relay(d, i) for i in range(VIA_NEXT, half)]
+        when(relay_ok(d) & relayed(d, i), act)
+
+    def turn(d, group, groups):
+        first = [lambda j=j: pass_on(d, j) for j in range(max(VIA_ROW, VIA_NEXT))]
+        then = [lambda j=j: relay(d, j) for j in range(min(VIA_ROW, VIA_NEXT), pieces)]
+        mixed = first[:1]
+        for j in range(max(len(first) - 1, len(then))):
+            mixed += first[j + 1 : j + 2] + then[j : j + 1]
         edge = x == d * (XS - 1)
-        when(edge, (then + first)[j])
-        when(jnp.logical_not(edge), (first + then)[j])
+
+        def act(order):
+            for one in order[group * len(order) // groups : (group + 1) * len(order) // groups]:
+                one()
+
+        when(edge, lambda: act(then + first))
+        when(jnp.logical_not(edge), lambda: act(mixed))
 
     def meta_copy(k):
         if k == 0:
@@ -218,9 +242,11 @@
             total = hi_part + jnp.where(l_lo == l_hi, lo_part, 0.0)
         else:
             total = lo_part + jnp.where(f_lo == f_hi, hi_part, 0.0)
-        tsend[d, i] = total
-        when(ok(d, 1), lambda: next_copy(d, i).start())
-        when(ok(d, 2) & (i >= VIA_NEXT), lambda: back_copy(d, i).start())
+        for k in range(PIECES):
+            j = i * PIECES + k
+            tsend[d, j] = total[k * depth : (k + 1) * depth]
+            when(ok(d, 1), lambda j=j: next_copy(d, j).start())
+            when(ok(d, 2) & sent_back(d, j), lambda j=j: back_copy(d, j).start())
 
     def fwd_total(i):
         sib_copy(0, i, own.at[other + i]).wait_recv()
@@ -278,12 +304,12 @@
         in_last = lab[...] == lab[tokens - 1 : tokens, :]
         vl[:, s] = jnp.where(in_last, va[:, s].astype(F32), 0.0).astype(BF16)
 
-    split = heads - half // 2 - 1
-    loop(split, inside)
-    for j in range(half):
-        turn(0, j)
-        if split + j < heads:
-            inside(split + j)
+    groups = half + 1
+    loop(heads - half, inside)
+    for group in range(groups):
+        turn(0, group, groups)
+        if group < half:
+            inside(heads - half + group)
     acc[...] = jnp.zeros_like(acc)
 
     for k, (back, slot) in enumerate(((2, 3), (3, 4), (0, 5), (1, 6))):
@@ -295,18 +321,24 @@
         when(jnp.logical_not(near_ok[back]), missing)
 
     def receive(d, i, finish):
-        when(ok(d, -1) & (i >= VIA_NEXT), lambda: next_copy(d, i).wait_recv())
-        when(ok(d, -2), lambda: relay_copy(d, i).wait_recv())
+        one, two = [], []
+        for k in range(PIECES):
+            j = i * PIECES + k
+            when(ok(d, -1) & jnp.logical_not(passed(d, j)), lambda j=j: next_copy(d, j).wait_recv())
+            when(ok(d, -2), lambda j=j: relay_copy(d, j).wait_recv())
+            one.append(tin[d, 0, j])
+            two.append(tin[d, 1, j])
+        one, two = jnp.concatenate(one, axis=0), jnp.concatenate(two, axis=0)
         a, b = own[mine + i], sib_in[d, i]
         lo_part, hi_part = jnp.where(lo, a, b), jnp.where(lo, b, a)
         if d == 0:
-            one, two = meta[3, 1:2, :] == f_lo, meta[4, 1:2, :] == f_lo
-            edge = jnp.where(one, tin[d, 0, i], 0.0) + jnp.where(two, tin[d, 1, i], 0.0)
+            one_ok, two_ok = meta[3, 1:2, :] == f_lo, meta[4, 1:2, :] == f_lo
+            edge = jnp.where(one_ok, one, 0.0) + jnp.where(two_ok, two, 0.0)
             inner = jnp.where(l_lo == f_hi, lo_part, 0.0) + jnp.where(f_lo == f_hi, edge, 0.0)
             to_lo, to_hi = edge, inner
         else:
-            one, two = meta[5, 0:1, :] == l_hi, meta[6, 0:1, :] == l_hi
-            edge = jnp.where(one, tin[d, 0, i], 0.0) + jnp.where(two, tin[d, 1, i], 0.0)
+            one_ok, two_ok = meta[5, 0:1, :] == l_hi, meta[6, 0:1, :] == l_hi
+            edge = jnp.where(one_ok, one, 0.0) + jnp.where(two_ok, two, 0.0)
             inner = jnp.where(f_hi == l_lo, hi_part, 0.0) + jnp.where(l_hi == l_lo, edge, 0.0)
             to_lo, to_hi = inner, edge
         sib_out[d, i] = jnp.where(lo, to_hi, to_lo)
@@ -337,6 +369,8 @@
 
     for k in range(n_head - 1):
         stat_copy(k).start()
+    for i in range(half):
+        sib_copy(0, i, own.at[other + i]).wait_send()
     for k in range(n_head - 1):
         stat_copy(k).wait_recv()
     rows = stat[0]
@@ -388,9 +422,6 @@
             mg[:, cols(h)] = m
             own[h] = part
 
-    for i in range(half):
-        sib_copy(0, i, own.at[other + i]).wait_send()
-
     def send_grad(j):
         grad_part(other + 2 * j, other + 2 * j + 1)
         for i in (2 * j, 2 * j + 1):
@@ -432,11 +463,10 @@
     loop(2, pair)
     gain_stage(0)
     loop(half - 2, lambda i: pair(2 + i))
-    turn(1, 0)
-    for j in range(1, half):
-        pair(half + j - 1)
-        turn(1, j)
-    pair(heads - 1)
+    for group in range(groups):
+        turn(1, group, groups)
+        if group < half:
+            pair(heads - half + group)
 
     def final(h):
         s = cols(h)
@@ -444,33 +474,34 @@
         kg_ref[:, s] = ((kp[:, s] + mm(vl[:, s], gb, 1, 1)) * sk[:, s]).astype(BF16)
         vg_ref[:, s] = ((vp[:, s] + mm(kl[:, s], gb, 1, 0)) * sv[:, s]).astype(BF16)
 
-    loop(half, lambda i: receive(1, i, final))
-    loop(half, lambda i: receive_sib(1, i, final))
-    gain_stage(1)
-
+    def drain(d):
+        def pieces_out(j):
+            when(ok(d, 1), lambda: next_copy(d, j).wait_send())
+            when(ok(d, 1) & ok(d, -1) & passed(d, j), lambda: pass_copy(d, j).wait_send())
+            when(ok(d, 2) & sent_back(d, j), lambda: back_copy(d, j).wait_send())
+            when(relay_ok(d) & relayed(d, j), lambda: relay_copy(d, j).wait_send())
+
+        loop(pieces, pieces_out)
+
+    drain(0)
+    loop(half, lambda i: sib_copy(0, half + i, sib_out.at[0, i]).wait_send())
+    loop(half, lambda i: sib_copy(1, i, own.at[other + i]).wait_send())
     meta_copy(0).wait_send()
     for k in range(1, 5):
         when(near_ok[k - 1], lambda k=k: meta_copy(k).wait_send())
     for k in range(n_head - 1):
         stat_copy(k).wait_send()
-    for stage in stages:
-        for cp in stage:
-            cp.wait_send()
-
-    def drain(i):
-        sib_copy(1, i, own.at[other + i]).wait_send()
-        for d in (0, 1):
-            sib_copy(d, half + i, sib_out.at[d, i]).wait_send()
-            when(ok(d, 1), lambda d=d: next_copy(d, i).wait_send())
-            when(ok(d, 1) & ok(d, -1) & (i < VIA_NEXT), lambda d=d: pass_copy(d, i).wait_send())
-
-            def relayed(d=d):
-                relay_copy(d, i).wait_send()
-
-            when(ok(d, 2) & (i >= VIA_NEXT), lambda d=d: back_copy(d, i).wait_send())
-            when(relay_ok(d) & (i >= VIA_NEXT), relayed)
-
-    loop(half, drain)
+    for cp in stages[0]:
+        cp.wait_send()
+    loop(half - 1, lambda i: receive(1, i, final))
+    drain(1)
+    receive(1, half - 1, final)
+    loop(half, lambda i: receive_sib(1, i, final))
+    gain_stage(1)
+
+    for cp in stages[1]:
+        cp.wait_send()
+    loop(half, lambda i: sib_copy(1, half + i, sib_out.at[1, i]).wait_send())
 
 
 def write_kernel(n, *refs):
@@ -503,6 +534,8 @@
     square = pltpu.VMEM((tokens, tokens), F32)
     thin = pltpu.VMEM((tokens, HD), F32)
     state = lambda *lead: pltpu.VMEM((*lead, HD, HD), F32)
+    piece = lambda *lead: pltpu.VMEM((*lead, HD // PIECES, HD), F32)
+    pieces = half * PIECES
     dma = pltpu.SemaphoreType.DMA
     n_gain = 1 + 2 * (XS - 1) + zs - 1
     vmem = pl.BlockSpec(memory_space=pltpu.VMEM)
@@ -517,14 +550,14 @@
         + [pltpu.VMEM((heads, tokens, tokens), BF16)] + [flat32] * 8
         + [pltpu.VMEM((width,), BF16), pltpu.VMEM((1, tokens), jnp.int32), pltpu.VMEM((heads, HD), F32), thin, square, pltpu.VMEM((2, tokens, HD), F32), thin, thin]
         + [
-            state(heads), state(2, half), state(2, 2 * half), state(2, half), state(2, 2, half), state(2, half),
+            state(heads), state(2, half), state(2, 2 * half), piece(2, pieces), piece(2, 2, pieces), piece(2, pieces),
             pltpu.VMEM((2, heads, HD, HD), BF16),
             pltpu.VMEM((7, 8, HD), F32),
             pltpu.VMEM((n_head, 8, tokens), F32),
             pltpu.VMEM((2 + n_gain, heads, HD), F32),
-            dma((7,)), dma((2, 2 * half)), dma((2, 2 * half)), dma((2, 2, half)), dma((2, 2, half)),
+            dma((7,)), dma((2, 2 * half)), dma((2, 2 * half)), dma((2, 2, pieces)), dma((2, 2, pieces)),
             dma((5,)), dma((5,)), dma((n_head - 1,)), dma((n_head - 1,)), dma((n_gain,)), dma((n_gain,)),
-            dma((2, half)), dma((2, half)), pltpu.SemaphoreType.REGULAR,
+            dma((2, pieces)), dma((2, pieces)), pltpu.SemaphoreType.REGULAR,
         ],
         compiler_params=pltpu.CompilerParams(
             collective_id=0, has_side_effects=True, vmem_limit_bytes=56 << 20

time: 43 us -> 42.4 us (0.986)
  the two profiles are of different devices: /device:TPU:1 before, /device:TPU:69 now
where the time goes in v5:
time: 42.4 us; the launch traced here: 42.3 us
  Pallas kernels  41.6 us (98%)
  between operations  0.64 us (2%)
    pallas_call x1, Pallas kernels, local(): pl.pallas_call(functools.partial(kernel, n_ctx, n_head, heads), out_shape...  40.1 us
    pallas_call x1, Pallas kernels, write_out(): pl.pallas_call(functools.partial(write_kernel, n), out_shape=tuple((jax.S...  1.54 us

profile of v5, /device:TPU:69, one launch (start us, length us, event | category | flops | bytes accessed | tf_op | source)
XLA Modules:
  0.0 42.3 jit_solution(12753941060768658001)
XLA Ops:
  0.6 40.1 %shard_map.118 = (bf16[256,1024]{1,0:T(8,128)(2,1)S(1)}, bf16[256,1024]{1,0:T(8,128)(2,1)S(1)}, bf16[256,1024]{1,0:T(8,128)(2,1)S(1)}, bf16[256,1024]{1,0:T(8,12...) custom-call(bf16[256,1024]{1,0:T(8,128)(2,1)} %xq_hbm.1, bf16[256,1024]{1,0:T(8,128)(2,1)} %xk_hbm.1, ...), custom_call_target="tpu_custom_call" | custom-call | flops 1073741824 | bytes 5242880 | tf_op jit(solution)/shard_map/pallas_call | solution.py:544
  40.7 1.5 %shard_map.119 = (bf16[256,1024]{1,0:T(8,128)(2,1)}, bf16[256,1024]{1,0:T(8,128)(2,1)}, bf16[256,1024]{1,0:T(8,128)(2,1)}, bf16[256,1024]{1,0:T(8,128)(2,1)}, bf...) custom-call(bf16[256,1024]{1,0:T(8,128)(2,1)S(1)} %get-tuple-element.18.refs_0_, ...), custom_call_target="tpu_custom_call" | custom-call | tf_op jit(solution)/shard_map/pallas_call | solution.py:518

commit v6 on v5

--- a/solution.py
+++ b/solution.py
@@ -407,9 +407,6 @@
         s = cols(h)
         gbuf[0, pl.ds(h, 1), :] = jnp.sum(ng[:, s] * mix[:, s] * inv_b[...], axis=0, keepdims=True)
 
-    loop(heads, gain_row)
-    for cp in stages[0]:
-        cp.start()
 
     def grad_part(*which):
         inv_r, cc_r = inv_b[...], cc_b[...]
@@ -428,6 +425,9 @@
             sib_copy(1, i, own.at[other + i]).start()
 
     loop(half // 2, send_grad)
+    loop(heads, gain_row)
+    for cp in stages[0]:
+        cp.start()
 
     def bwd_total(j):
         grad_part(mine + 2 * j, mine + 2 * j + 1)

time: 42.4 us -> 41.9 us (0.988)
  the two profiles are of different devices: /device:TPU:69 before, /device:TPU:1 now
where the time goes in v6:
time: 41.9 us; the launch traced here: 41.2 us
  Pallas kernels  40.5 us (97%)
  between operations  0.64 us (2%)
    pallas_call x1, Pallas kernels, local(): pl.pallas_call(functools.partial(kernel, n_ctx, n_head, heads), out_shape...  39 us
    pallas_call x1, Pallas kernels, write_out(): pl.pallas_call(functools.partial(write_kernel, n), out_shape=tuple((jax.S...  1.54 us

profile of v6, /device:TPU:1, one launch (start us, length us, event | category | flops | bytes accessed | tf_op | source)
XLA Modules:
  0.0 41.2 jit_solution(1722094400469335818)
XLA Ops:
  0.6 39.0 %shard_map.118 = (bf16[256,1024]{1,0:T(8,128)(2,1)S(1)}, bf16[256,1024]{1,0:T(8,128)(2,1)S(1)}, bf16[256,1024]{1,0:T(8,128)(2,1)S(1)}, bf16[256,1024]{1,0:T(8,12...) custom-call(bf16[256,1024]{1,0:T(8,128)(2,1)} %xq_hbm.1, bf16[256,1024]{1,0:T(8,128)(2,1)} %xk_hbm.1, ...), custom_call_target="tpu_custom_call" | custom-call | flops 1073741824 | bytes 5242880 | tf_op jit(solution)/shard_map/pallas_call | solution.py:544
  39.6 1.5 %shard_map.119 = (bf16[256,1024]{1,0:T(8,128)(2,1)}, bf16[256,1024]{1,0:T(8,128)(2,1)}, bf16[256,1024]{1,0:T(8,128)(2,1)}, bf16[256,1024]{1,0:T(8,128)(2,1)}, bf...) custom-call(bf16[256,1024]{1,0:T(8,128)(2,1)S(1)} %get-tuple-element.18.refs_0_, ...), custom_call_target="tpu_custom_call" | custom-call | tf_op jit(solution)/shard_map/pallas_call | solution.py:518

commit v7 on v6

--- a/solution.py
+++ b/solution.py
@@ -81,9 +81,9 @@
     for i, (src, dst) in enumerate(
         ((doc_hbm, docs), (xk_hbm, xk), (xv_hbm, xv), (xq_hbm, xq), (gl_hbm, gl), (og_hbm, og), (gain_hbm, gain16))
     ):
-        cp = pltpu.make_async_copy(src, dst, in_sem.at[i])
-        cp.start()
-        loads.append(cp)
+        loads.append(pltpu.make_async_copy(src, dst, in_sem.at[i]))
+    for load in loads[:3]:
+        load.start()
     barrier = pltpu.get_barrier_semaphore()
     greeted = jnp.int32(len(always))
     for q in always:
@@ -91,6 +91,8 @@
     for q, there in chain + ([(across, lead)] if zs > quad else []):
         when(there, lambda q=q: pl.semaphore_signal(barrier, inc=1, device_id=q, device_id_type=MESH))
         greeted = greeted + there.astype(jnp.int32)
+    for load in loads[3:]:
+        load.start()
 
     def remote(src, dst, ssem, rsem, dev):
         return pltpu.make_async_remote_copy(

time: 41.9 us -> 41.9 us (level)
  no operation moved by 1% of the time
where the time goes in v7:
time: 41.9 us; the launch traced here: 41.2 us
  Pallas kernels  40.5 us (97%)
  between operations  0.64 us (2%)
    pallas_call x1, Pallas kernels, local(): pl.pallas_call(functools.partial(kernel, n_ctx, n_head, heads), out_shape...  39 us
    pallas_call x1, Pallas kernels, write_out(): pl.pallas_call(functools.partial(write_kernel, n), out_shape=tuple((jax.S...  1.54 us

profile of v7, /device:TPU:1, one launch (start us, length us, event | category | flops | bytes accessed | tf_op | source)
XLA Modules:
  0.0 41.2 jit_solution(1324204686916194989)
XLA Ops:
  0.6 39.0 %shard_map.118 = (bf16[256,1024]{1,0:T(8,128)(2,1)S(1)}, bf16[256,1024]{1,0:T(8,128)(2,1)S(1)}, bf16[256,1024]{1,0:T(8,128)(2,1)S(1)}, bf16[256,1024]{1,0:T(8,12...) custom-call(bf16[256,1024]{1,0:T(8,128)(2,1)} %xq_hbm.1, bf16[256,1024]{1,0:T(8,128)(2,1)} %xk_hbm.1, ...), custom_call_target="tpu_custom_call" | custom-call | flops 1073741824 | bytes 5242880 | tf_op jit(solution)/shard_map/pallas_call | solution.py:546
  39.6 1.5 %shard_map.119 = (bf16[256,1024]{1,0:T(8,128)(2,1)}, bf16[256,1024]{1,0:T(8,128)(2,1)}, bf16[256,1024]{1,0:T(8,128)(2,1)}, bf16[256,1024]{1,0:T(8,128)(2,1)}, bf...) custom-call(bf16[256,1024]{1,0:T(8,128)(2,1)S(1)} %get-tuple-element.18.refs_0_, ...), custom_call_target="tpu_custom_call" | custom-call | tf_op jit(solution)/shard_map/pallas_call | solution.py:520
